TPU v7x, 768 devices: a whole 4x8x12 slice. The times are simulated.
768 devices in a mesh: grp: 12 (over z), rep: 64 (over y, x, core).
Axes of the slice: x: 4, y: 8, z: 12, core: 2. Of those that a mesh axis runs over, the one named last changes fastest.
Arguments:
- grid: bfloat16 [64, 12, 192, 512], P('rep', 'grp'), may hold values from -6 to 6
- cotangent: bfloat16 [64, 12, 192, 512], P('rep', 'grp'), may hold values from -6 to 6
- send_order: int32 [64, 12, 192], P('rep', 'grp'), may hold values from 0 to 191, each once within a row
- tile_nodes: int32 [64, 12, 24, 64], P('rep', 'grp'), may hold values from 0 to 191
- tile_edges: int32 [64, 12, 24, 64, 64], P('rep', 'grp'), may hold values 0 or 1
- tile_count: int32 [64, 12], P('rep', 'grp'), may hold values from 1 to 24, as said below
- w_first: bfloat16 [512, 512], replicated, may hold values from -0.25 to 0.25
- w_second: bfloat16 [512, 512], replicated, may hold values from -0.25 to 0.25
Outputs:
- grad_grid: bfloat16 [64, 12, 192, 512], P('rep', 'grp')
- grad_first: float32 [512, 512], replicated
- grad_second: float32 [512, 512], replicated
Inputs may be any that keep to these rules, and one draw needn't show every extreme that they name: `tile_count`: every device uses at least one tile, and some device uses exactly 24.
All inputs are finite; a program needn't handle non-finite values. No bound on the sum of `tile_edges` on one device may be relied on, other than what follows from the above.
Results may differ from a plain program's by a relative error of at most 0.0055.
Values may be sent and summed in bfloat16 or wider, within the bound.
No kernel may reach another device: no remote copies, remote signals or barrier semaphores. Data moves between devices by JAX's collectives and lax.ppermute only.
A program may use at most 32 MiB of HBM per device.

v0:
```python
import jax
import jax.numpy as jnp
from jax import lax
from jax.sharding import PartitionSpec as P


def shards(grid, cotangent, send_order, tile_nodes, tile_edges, tile_count, w_first, w_second):
    rows = grid[0, 0]
    order = send_order[0, 0]
    parts_here = lax.axis_size("grp")
    nodes_dev = rows.shape[0]
    width = rows.shape[1]
    share = nodes_dev // parts_here
    outgoing = jnp.take(rows, order, axis=0).reshape(parts_here, share, width)
    incoming = lax.all_to_all(outgoing, "grp", split_axis=0, concat_axis=0, tiled=True)
    part = incoming.reshape(nodes_dev, width)
    nodes = tile_nodes[0, 0]
    most = nodes.shape[0]
    tile = nodes.shape[1]
    valid = (jnp.arange(most) < tile_count[0, 0]).astype(jnp.bfloat16)
    edges = tile_edges[0, 0].astype(jnp.bfloat16) * valid[:, None, None]
    flat = nodes.reshape(-1)
    slots = flat.shape[0]
    hin = jnp.take(part, flat, axis=0)
    pre = jnp.dot(hin, w_first, preferred_element_type=jnp.float32)
    act = jax.nn.silu(pre).astype(jnp.bfloat16).reshape(most, tile, width)
    agg = jnp.einsum("bij,bjd->bid", edges, act, preferred_element_type=jnp.float32)
    agg = agg.astype(jnp.bfloat16).reshape(slots, width)
    dy = jnp.take(cotangent[0, 0], flat, axis=0)
    local_second = jnp.einsum("sd,se->de", agg, dy, preferred_element_type=jnp.float32)
    dagg = jnp.einsum("se,de->sd", dy, w_second, preferred_element_type=jnp.float32).astype(
        jnp.bfloat16
    )
    dact = jnp.einsum(
        "bij,bid->bjd", edges, dagg.reshape(most, tile, width), preferred_element_type=jnp.float32
    )
    dact = dact.reshape(slots, width)
    sig = jax.nn.sigmoid(pre)
    dpre = (dact * sig * (1.0 + pre * (1.0 - sig))).astype(jnp.bfloat16)
    local_first = jnp.einsum("sd,se->de", hin, dpre, preferred_element_type=jnp.float32)
    dh = jnp.einsum("se,de->sd", dpre, w_first, preferred_element_type=jnp.float32)
    onehot = (flat[:, None] == jnp.arange(nodes_dev, dtype=jnp.int32)[None, :]).astype(jnp.float32)
    dpart = jnp.einsum(
        "sn,sd->nd", onehot, dh, precision=lax.Precision.HIGHEST, preferred_element_type=jnp.float32
    )
    dpart = dpart.astype(jnp.bfloat16)
    returned = lax.all_to_all(
        dpart.reshape(parts_here, share, width), "grp", split_axis=0, concat_axis=0, tiled=True
    )
    inverse = jnp.argsort(order, stable=True)
    grad_rows = jnp.take(returned.reshape(nodes_dev, width), inverse, axis=0)
    total_first, total_second = lax.psum((local_first, local_second), ("grp", "rep"))
    factor = float(lax.axis_size("grp") * lax.axis_size("rep") * most * tile) ** (-0.5)
    return (grad_rows[None, None], total_first * factor, total_second * factor)


def solution(mesh):
    in_specs = (
        P("rep", "grp", None, None),
        P("rep", "grp", None, None),
        P("rep", "grp", None),
        P("rep", "grp", None, None),
        P("rep", "grp", None, None, None),
        P("rep", "grp"),
        P(),
        P(),
    )
    out_specs = (P("rep", "grp", None, None), P(), P())
    return jax.shard_map(shards, mesh=mesh, in_specs=in_specs, out_specs=out_specs, check_vma=False)
```

profile of v0, /device:TPU:1, one launch (start us, length us, event | category | flops | bytes accessed | tf_op | source)
XLA Modules:
  0.0 558.0 jit_solution(15761207521824176951)
XLA Ops:
  7.2 0.0 copy-start
  7.2 0.0 copy-start.4
  7.2 0.0 copy-start.1
  7.2 0.7 compare_select_fusion.2
  7.9 0.7 compare_and_fusion.2
  8.6 2.0 gather_fusion.1
  10.6 0.8 broadcast_select_fusion.6
  11.4 15.7 %all-to-all-start = ((bf16[12,16,512]{2,1,0:T(8,128)(2,1)}), bf16[12,16,512]{2,1,0:T(8,128)(2,1)S(1)}, u32[]{:S(2)}, u32[]{:S(2)}) async-start(bf16[12,16,512]{2,1,0:T(8,128)(2,1)} %bitcast.7), calls=%async_computation | async-start | bytes 393216 | tf_op jit(solution)/shard_map/all_to_all | solution.py:15
  27.1 0.0 all-reduce.3.cloned.1.call-start
  27.2 0.0 copy-done.4
  27.2 0.1 eq.15
  27.3 0.0 copy-done.1
  27.3 4.8 gather_fusion
  32.1 0.0 copy-start.5
  32.1 0.0 copy-start.2
  32.1 3.3 convolution_convert_fusion
  36.1 0.0 copy-done.5
  36.1 3.2 sort.17
  39.3 0.0 copy-done.2
  39.3 4.0 fusion.12
  43.3 0.0 all-to-all-done
  43.3 5.4 gather_fusion.2
  48.7 0.0 copy-done
  48.7 0.0 copy-start.3
  48.7 4.6 multiply_convert_fusion
  53.4 0.0 copy-done.3
  53.4 2.1 fusion.6
  55.5 2.7 fusion.13
  58.2 0.6 convolution_convert_fusion.1
  58.8 2.1 fusion.5
  60.9 0.0 all-reduce.3.cloned.1.call-update
  60.9 4.7 fusion.3
  65.5 9.0 %all-to-all-start.1 = ((bf16[12,16,512]{2,1,0:T(8,128)(2,1)}), bf16[12,16,512]{2,1,0:T(8,128)(2,1)S(1)}, u32[]{:S(2)}, u32[]{:S(2)}) async-start(bf16[12,16,512]{2,1,0:T(8,128)(2,1)} %bitcast.9), calls=%async_computation.1 | async-start | bytes 393216 | tf_op jit(solution)/shard_map/all_to_all | solution.py:47
  74.6 11.5 %all-to-all-done.1 = bf16[12,16,512]{2,1,0:T(8,128)(2,1)S(1)} async-done(((bf16[12,16,512]{2,1,0:T(8,128)(2,1)}), bf16[12,16,512]{2,1,0:T(8,128)(2,1)S(1)}, u32[]{:S(2)}, u32[]{:S(2)}) %all-to-all-start.1) | async-done | bytes 196640 | tf_op jit(solution)/shard_map/all_to_all | solution.py:47
  86.1 1.0 gather_fusion.3
  87.1 0.8 select_bitcast_fusion
  87.8 460.3 %all-reduce.3.cloned.1.call-done = (f32[512,512]{1,0:T(8,128)}, f32[512,512]{1,0:T(8,128)}) async-done(((f32[512,512]{1,0:T(8,128)}, f32[512,512]{1,0:T(8,128)}), (f32[512,512]{1,0:T(8,128)}, f32[512,512]{1,0:T(8,128)})) %all-reduce.3.cloned.1.call-update) | async-done | bytes 2097168 | tf_op jit(solution)/shard_map/psum | solution.py:52
  548.1 3.1 broadcast_multiply_fusion
  (9 shorter events, 0.1 us)
Async XLA Ops:
  7.2 41.6 %copy-start = (bf16[512,512]{1,0:T(8,128)(2,1)S(1)}, bf16[512,512]{1,0:T(8,128)(2,1)}, u32[]{:S(2)}) copy-start(bf16[512,512]{1,0:T(8,128)(2,1)} %param.18) | copy-start | bytes 1572868
  7.2 20.0 %copy-start.4 = (s32[1,1,24,64]{3,2,1,0:T(8,128)S(1)}, s32[1,1,24,64]{3,2,1,0:T(8,128)}, u32[]{:S(2)}) copy-start(s32[1,1,24,64]{3,2,1,0:T(8,128)} %param.15) | copy-start | bytes 18436
  7.2 20.1 %copy-start.1 = (bf16[1,1,192,512]{3,2,1,0:T(8,128)(2,1)S(1)}, bf16[1,1,192,512]{3,2,1,0:T(8,128)(2,1)}, u32[]{:S(2)}) copy-start(bf16[1,1,192,512]{3,2,1,0:T(8,128)(2,1)} %param.13) | copy-start | bytes 589828
  11.4 31.9 %all-to-all-start = ((bf16[12,16,512]{2,1,0:T(8,128)(2,1)}), bf16[12,16,512]{2,1,0:T(8,128)(2,1)S(1)}, u32[]{:S(2)}, u32[]{:S(2)}) async-start(bf16[12,16,512]{2,1,0:T(8,128)(2,1)} %bitcast.7), calls=%async_computation | async-start | bytes 393216 | tf_op jit(solution)/shard_map/all_to_all | solution.py:15
  27.1 521.0 %all-reduce.3.cloned.1.call-start = ((), (), s32[]{:S(2)}) async-start(), calls=%async_computation.2 | async-start | bytes 4194304 | tf_op jit(solution)/shard_map/psum | solution.py:52
  32.1 4.0 copy-start.5
  32.1 7.2 %copy-start.2 = (s32[1,1,24,64,64]{4,3,2,1,0:T(8,128)S(1)}, s32[1,1,24,64,64]{4,3,2,1,0:T(8,128)}, u32[]{:S(2)}) copy-start(s32[1,1,24,64,64]{4,3,2,1,0:T(8,128)} %param.16) | copy-start | bytes 1179652
  48.7 4.6 copy-start.3
  65.5 20.5 %all-to-all-start.1 = ((bf16[12,16,512]{2,1,0:T(8,128)(2,1)}), bf16[12,16,512]{2,1,0:T(8,128)(2,1)S(1)}, u32[]{:S(2)}, u32[]{:S(2)}) async-start(bf16[12,16,512]{2,1,0:T(8,128)(2,1)} %bitcast.9), calls=%async_computation.1 | async-start | bytes 393216 | tf_op jit(solution)/shard_map/all_to_all | solution.py:47
Sparse Core Ops, SparseCore 0:
  61.0 487.0 all-reduce.2
where the time goes:
time: 560 us; the launch traced here: 558 us
  waiting for transfers between devices  472 us (84%)
  starting transfers between devices  24.7 us (4%)
  matrix products  24.1 us (4%)
  between operations  14.8 us (3%)
  local copies, waits for them, and re-layouts  13.3 us (2%)
  other arithmetic  9.3 us (2%)
    psum x1, waiting for transfers between devices, shards(): lax.psum((local_first, local_second), ('grp', 'rep'))  460 us
    all_to_all x1, starting transfers between devices, shards(): lax.all_to_all(outgoing, 'grp', split_axis=0, concat_axis=0, tiled=True)  15.7 us
    all_to_all x1, waiting for transfers between devices, shards(): lax.all_to_all(dpart.reshape(parts_here, share, width), 'grp', split_axis...  11.5 us
  transfers between devices with their start and end apart: 3, of which 2 were waited for; matrix products, arithmetic and copies ran while one was open for 4% of the time, Pallas kernels for 0%

commit v1 on v0

v1 whole, which is shorter than its diff:
```python
import jax
import jax.numpy as jnp
from jax import lax
from jax.experimental import pallas as pl
from jax.experimental.pallas import tpu as pltpu
from jax.sharding import Mesh, PartitionSpec as P

BF = jnp.bfloat16
F32 = jnp.float32
NT = (((1,), (1,)), ((), ()))
TN = (((0,), (0,)), ((), ()))


def dot(a, b):
    return jnp.dot(a, b, preferred_element_type=F32)


def dot_nt(a, b):
    return lax.dot_general(a, b, NT, preferred_element_type=F32)


def dot_tn(a, b):
    return lax.dot_general(a, b, TN, preferred_element_type=F32)


def mark(hit):
    return jnp.where(hit, 1.0, 0.0).astype(BF)


def split(a):
    high = a.astype(BF)
    return high, (a - high.astype(F32)).astype(BF)


def send_kernel(order_ref, rows_ref, out_ref):
    n = rows_ref.shape[0]
    places = mark(lax.broadcasted_iota(jnp.int32, (n, n), 0) == order_ref[...])
    out_ref[...] = dot_tn(places, rows_ref[...]).astype(BF)


def local_kernel(count_ref, nodes_ref, edges_ref, cot_ref, w2_ref, high_ref, low_ref, t_ref):
    most, tile = nodes_ref.shape
    n = cot_ref.shape[0]
    count = count_ref[0, 0]
    ids = lax.broadcasted_iota(jnp.int32, (n, tile), 0)
    total = jnp.zeros((n, n), F32)
    for b in range(most):
        used = jnp.where(b < count, 1.0, 0.0)
        at = mark(ids == nodes_ref[b : b + 1, :])
        edges = (edges_ref[b].astype(F32) * used).astype(BF)
        total = total + dot_nt(dot(at, edges).astype(BF), at)
    high, low = split(total)
    high_ref[...] = high
    low_ref[...] = low
    dagg = dot_nt(cot_ref[...], w2_ref[...]).astype(BF)
    t_ref[...] = dot_tn(high, dagg) + dot_tn(low, dagg)


def node_kernel(factor, part_ref, w1_ref, cot_ref, high_ref, low_ref, t_ref, grads_ref, dpart_ref):
    d = w1_ref.shape[0]
    part = part_ref[...]
    pre = dot(part, w1_ref[...])
    sig = jax.nn.sigmoid(pre)
    act = (pre * sig).astype(BF)
    g = (t_ref[...] * sig * (1.0 + pre * (1.0 - sig))).astype(BF)
    dpart_ref[...] = dot_nt(g, w1_ref[...]).astype(BF)
    grads_ref[0:d, :] = (dot_tn(part, g) * factor).astype(BF)
    m = (dot(high_ref[...], act) + dot(low_ref[...], act)).astype(BF)
    grads_ref[d : 2 * d, :] = (dot_tn(m, cot_ref[...]) * factor).astype(BF)


def sum_kernel(pieces_ref, dpart_ref, both_ref):
    z, share, _ = dpart_ref.shape
    total = jnp.sum(pieces_ref[...].astype(F32), axis=0).astype(BF)
    for k in range(z):
        both_ref[k, 0:share, :] = dpart_ref[k]
        both_ref[k, share:, :] = total


def spread_kernel(both_ref, back_ref, whole_ref):
    z, share, _ = back_ref.shape
    back_ref[...] = both_ref[:, 0:share, :]
    total = jnp.sum(both_ref[:, share:, :].astype(F32), axis=0).astype(BF)
    for k in range(whole_ref.shape[0]):
        whole_ref[k] = total


def place_kernel(order_ref, back_ref, out_ref):
    n = back_ref.shape[0]
    places = mark(lax.broadcasted_iota(jnp.int32, (n, n), 0) == order_ref[...])
    out_ref[...] = dot(places, back_ref[...]).astype(BF)


def call(kernel, out_shape, flops, nbytes, *args, smem=0):
    specs = [pl.BlockSpec(memory_space=pltpu.SMEM)] * smem
    specs += [pl.BlockSpec(memory_space=pltpu.VMEM)] * (len(args) - smem)
    return pl.pallas_call(
        kernel,
        out_shape=out_shape,
        in_specs=specs,
        compiler_params=pltpu.CompilerParams(vmem_limit_bytes=32 * 1024 * 1024),
        cost_estimate=pl.CostEstimate(flops=flops, bytes_accessed=nbytes, transcendentals=0),
    )(*args)


def shards(grid, cotangent, send_order, tile_nodes, tile_edges, tile_count, w_first, w_second):
    rows, cot, order = grid[0, 0], cotangent[0, 0], send_order[0]
    nodes, edges = tile_nodes[0, 0], tile_edges[0, 0]
    z = lax.axis_size("grp")
    rep = lax.axis_size("rep")
    n, d = rows.shape
    most, tile = nodes.shape
    factor = float(z * rep * most * tile) ** -0.5
    sd = jax.ShapeDtypeStruct

    outgoing = call(send_kernel, sd((n, d), BF), 2 * n * n * d, 4 * n * d, order, rows)
    incoming = lax.all_to_all(outgoing.reshape(z, n // z, d), "grp", 0, 0, tiled=True)
    part = incoming.reshape(n, d)

    high, low, t = call(
        local_kernel,
        (sd((n, n), BF), sd((n, n), BF), sd((n, d), F32)),
        10**9, 6 * 10**6, tile_count, nodes, edges, cot, w_second, smem=1,
    )
    grads, dpart = call(
        lambda *refs: node_kernel(factor, *refs),
        (sd((2 * d, d), BF), sd((n, d), BF)),
        5 * 10**8, 3 * 10**6, part, w_first, cot, high, low, t,
    )

    share = 2 * d // rep
    pieces = lax.all_to_all(grads.reshape(rep, share, d), "rep", 0, 0, tiled=True)
    both = call(
        sum_kernel, sd((z, n // z + share, d), BF), 10**6, 2 * 10**6,
        pieces, dpart.reshape(z, n // z, d),
    )
    both = lax.all_to_all(both, "grp", 0, 0, tiled=True)
    back, whole = call(
        spread_kernel, (sd((z, n // z, d), BF), sd((rep, share, d), BF)), 10**6, 2 * 10**6, both
    )
    whole = lax.all_to_all(whole, "rep", 0, 0, tiled=True).reshape(2 * d, d)
    grad_rows = call(place_kernel, sd((n, d), BF), 2 * n * n * d, 4 * n * d, order, back.reshape(n, d))
    return (grad_rows[None, None], whole[:d].astype(F32), whole[d:].astype(F32))


def solution(mesh):
    in_specs = (
        P("rep", "grp", None, None),
        P("rep", "grp", None, None),
        P("rep", "grp", None),
        P("rep", "grp", None, None),
        P("rep", "grp", None, None, None),
        P("rep", "grp"),
        P(),
        P(),
    )
    out_specs = (P("rep", "grp", None, None), P(), P())
    return jax.shard_map(shards, mesh=mesh, in_specs=in_specs, out_specs=out_specs, check_vma=False)
```

time: 560 us -> 133 us (0.24)
  waiting for transfers between devices: 472 us -> 34.1 us
  blocking collectives: 0 us -> 60.3 us
  matrix products: 24.1 us -> 0 us
  between operations: 14.8 us -> 1.35 us
  local copies, waits for them, and re-layouts: 13.3 us -> 4.35 us
  other arithmetic: 9.3 us -> 1.68 us
  Pallas kernels: 0 us -> 6.09 us
    psum x1 -> x0, waiting for transfers between devices: 460 us -> none  [shards(): lax.psum((local_first, local_second), ('grp', 'rep'))]
    all_to_all x0 -> x2, blocking collectives: none -> 60.3 us  [the longest x1 40.6 us: shards(): lax.all_to_all(grads.reshape(rep, share, d), 'rep', 0, 0, tiled=True)]
    dot_general x8 -> x0, matrix products: 24.1 us -> none  [the longest x1 4.65 us: shards(): jnp.einsum('sn,sd->nd', onehot, dh, precision=lax.Precision.HIGHEST, pref...]
    all_to_all x2, waiting for transfers between devices: 11.5 us -> 34.1 us  [the longest x1 27.1 us: shards(): whole = lax.all_to_all(whole, 'rep', 0, 0, tiled=True).reshape(2 * d, d)]
    gather x4 -> x0, local copies, waits for them, and re-layouts: 13.2 us -> none  [the longest x1 5.42 us: shards(): hin = jnp.take(part, flat, axis=0)]
    pallas_call x0 -> x6, Pallas kernels: none -> 6.09 us  [call(): pl.pallas_call(kernel, out_shape=out_shape, in_specs=specs, compiler_para...]
  transfers between devices with their start and end apart: 3 -> 2, of which waited for: 2 -> 2; matrix products, arithmetic and copies ran while one was open for 4% -> 0% of each run, Pallas kernels for 0% -> 2%
where the time goes in v1:
time: 133 us
  blocking collectives  60.3 us (45%)
  waiting for transfers between devices  34.1 us (26%)
  starting transfers between devices  25.1 us (19%)
  Pallas kernels  6.09 us (5%)
  local copies, waits for them, and re-layouts  4.35 us (3%)
  other arithmetic  1.68 us (1%)
  between operations  1.35 us (1%)
    all_to_all x1, blocking collectives, shards(): lax.all_to_all(grads.reshape(rep, share, d), 'rep', 0, 0, tiled=True)  40.6 us
    all_to_all x1, waiting for transfers between devices, shards(): whole = lax.all_to_all(whole, 'rep', 0, 0, tiled=True).reshape(2 * d, d)  27.1 us
    all_to_all x1, blocking collectives, shards(): both = lax.all_to_all(both, 'grp', 0, 0, tiled=True)  19.7 us
    all_to_all x1, starting transfers between devices, shards(): lax.all_to_all(outgoing.reshape(z, n // z, d), 'grp', 0, 0, tiled=True)  15.7 us
    all_to_all x1, starting transfers between devices, shards(): whole = lax.all_to_all(whole, 'rep', 0, 0, tiled=True).reshape(2 * d, d)  9.35 us
    all_to_all x1, waiting for transfers between devices, shards(): lax.all_to_all(outgoing.reshape(z, n // z, d), 'grp', 0, 0, tiled=True)  6.97 us
    pallas_call x6, Pallas kernels, call(): pl.pallas_call(kernel, out_shape=out_shape, in_specs=specs, compiler_para...  6.09 us
    unnamed x16, local copies, waits for them, and re-layouts  4.28 us
  transfers between devices with their start and end apart: 2, of which 2 were waited for; matrix products, arithmetic and copies ran while one was open for 0% of the time, Pallas kernels for 2%

profile of v1, /device:TPU:1, one launch (start us, length us, event | category | flops | bytes accessed | tf_op | source)
XLA Modules:
  0.0 132.8 jit_solution(6303253720147467226)
XLA Ops:
  0.6 0.0 copy-start.1
  0.6 0.7 copy-done.1
  1.3 0.0 copy-start
  1.3 0.9 copy-done
  2.2 0.0 copy-start.2
  2.2 0.9 shard_map.103
  3.2 15.7 %all-to-all-start = ((bf16[12,16,512]{2,1,0:T(8,128)(2,1)}), bf16[12,16,512]{2,1,0:T(8,128)(2,1)S(1)}, u32[]{:S(2)}, u32[]{:S(2)}) async-start(bf16[12,16,512]{2,1,0:T(8,128)(2,1)} %bitcast.2), calls=%async_computation | async-start | bytes 393216 | tf_op jit(solution)/shard_map/all_to_all | solution.py:117
  19.5 0.0 copy-done.2
  19.5 0.0 copy-start.3
  19.5 1.0 copy-done.3
  20.6 0.0 copy-start.5
  20.6 0.9 copy-done.5
  21.5 0.0 copy-start.7
  21.5 0.7 copy-done.7
  22.2 0.0 copy-start.4
  22.2 0.0 copy-start.6
  22.2 1.9 %shard_map.104 = (bf16[192,192]{1,0:T(8,128)(2,1)S(1)}, bf16[192,192]{1,0:T(8,128)(2,1)S(1)}, f32[192,512]{1,0:T(8,128)S(1)}) custom-call(s32[1,1]{1,0:T(1,128)S(6)} %copy.11.count_ref, s32[24,64]{1,0:T(8,128)S(1)} %bitcast.27, s32[24,64,64]{2,1,0:T(8,128)S(1)} %bitcast.24, bf16[192,512]{1,0:T(8,128)(2,1)S(1)} %bitcast.25, bf16[512,512]{1,0:T(8,128)(2,1)S(1)} %copy-done.3), custom_call_target="tpu_custom_call" | custom-call | flops 1000000000 | bytes 6000000 | tf_op jit(solution)/shard_map/pallas_call | solution.py:97
  24.2 7.0 %all-to-all-done = bf16[12,16,512]{2,1,0:T(8,128)(2,1)S(1)} async-done(((bf16[12,16,512]{2,1,0:T(8,128)(2,1)}), bf16[12,16,512]{2,1,0:T(8,128)(2,1)S(1)}, u32[]{:S(2)}, u32[]{:S(2)}) %all-to-all-start) | async-done | bytes 196640 | tf_op jit(solution)/shard_map/all_to_all | solution.py:117
  31.1 0.0 copy-done.4
  31.1 0.0 copy-done.6
  31.1 1.1 shard_map.105
  32.2 40.6 %all_to_all.20.pieces_ref = bf16[64,16,512]{2,1,0:T(8,128)(2,1)S(1)} all-to-all(bf16[64,16,512]{2,1,0:T(8,128)(2,1)S(1)} %bitcast.17), channel_id=1, replica_groups=mesh['grp'=12,'rep'=64] {'rep'}, dimensions={0} | all-to-all | bytes 2097152 | tf_op jit(solution)/shard_map/all_to_all | solution.py:132
  72.8 0.2 shard_map.106
  72.9 19.7 %all_to_all.21.both_ref = bf16[12,32,512]{2,1,0:T(8,128)(2,1)S(1)} all-to-all(bf16[12,32,512]{2,1,0:T(8,128)(2,1)S(1)} %shard_map.106), channel_id=1, replica_groups=mesh['grp'=12,'rep'=64] {'grp'}, dimensions={0} | all-to-all | bytes 786432 | tf_op jit(solution)/shard_map/all_to_all | solution.py:137
  92.6 1.1 shard_map.107
  93.7 9.3 %all-to-all-start.3 = ((bf16[64,16,512]{2,1,0:T(8,128)(2,1)}), bf16[64,16,512]{2,1,0:T(8,128)(2,1)S(1)}, u32[]{:S(2)}, u32[]{:S(2)}) async-start(bf16[64,16,512]{2,1,0:T(8,128)(2,1)} %get-tuple-element.16), calls=%async_computation.3 | async-start | bytes 2097152 | tf_op jit(solution)/shard_map/all_to_all | solution.py:141
  103.1 0.9 shard_map.108
  104.0 27.1 %all-to-all-done.3 = bf16[64,16,512]{2,1,0:T(8,128)(2,1)S(1)} async-done(((bf16[64,16,512]{2,1,0:T(8,128)(2,1)}), bf16[64,16,512]{2,1,0:T(8,128)(2,1)S(1)}, u32[]{:S(2)}, u32[]{:S(2)}) %all-to-all-start.3) | async-done | bytes 1048608 | tf_op jit(solution)/shard_map/all_to_all | solution.py:141
  131.1 0.1 fusion
  131.2 1.7 %bitcast_convert_fusion = (f32[512,512]{1,0:T(8,128)}, f32[512,512]{1,0:T(8,128)}) fusion(bf16[32,16,512]{2,1,0:T(8,128)(2,1)S(1)} %get-tuple-element.17, bf16[32,16,512]{2,1,0:T(8,128)(2,1)S(1)} %get-tuple-element.18), kind=kLoop, calls=%fused_computation | loop fusion | flops 524288 | bytes 3145728 | tf_op jit(solution)/shard_map/convert_element_type | solution.py:143
Async XLA Ops:
  0.6 0.7 copy-start.1
  1.3 0.9 copy-start
  2.2 17.3 %copy-start.2 = (s32[1,1,24,64,64]{4,3,2,1,0:T(8,128)S(1)}, s32[1,1,24,64,64]{4,3,2,1,0:T(8,128)}, u32[]{:S(2)}) copy-start(s32[1,1,24,64,64]{4,3,2,1,0:T(8,128)} %param.12) | copy-start | bytes 1179652
  3.2 28.0 %all-to-all-start = ((bf16[12,16,512]{2,1,0:T(8,128)(2,1)}), bf16[12,16,512]{2,1,0:T(8,128)(2,1)S(1)}, u32[]{:S(2)}, u32[]{:S(2)}) async-start(bf16[12,16,512]{2,1,0:T(8,128)(2,1)} %bitcast.2), calls=%async_computation | async-start | bytes 393216 | tf_op jit(solution)/shard_map/all_to_all | solution.py:117
  19.5 1.0 copy-start.3
  20.6 0.9 copy-start.5
  21.5 0.7 copy-start.7
  22.2 8.9 %copy-start.4 = (bf16[512,512]{1,0:T(8,128)(2,1)S(1)}, bf16[512,512]{1,0:T(8,128)(2,1)}, u32[]{:S(2)}) copy-start(bf16[512,512]{1,0:T(8,128)(2,1)} %refs_1_.1) | copy-start | bytes 1572868
  22.2 8.9 %copy-start.6 = (bf16[1,1,192,512]{3,2,1,0:T(8,128)(2,1)S(1)}, bf16[1,1,192,512]{3,2,1,0:T(8,128)(2,1)}, u32[]{:S(2)}) copy-start(bf16[1,1,192,512]{3,2,1,0:T(8,128)(2,1)} %param.9) | copy-start | bytes 589828
  93.7 37.3 %all-to-all-start.3 = ((bf16[64,16,512]{2,1,0:T(8,128)(2,1)}), bf16[64,16,512]{2,1,0:T(8,128)(2,1)S(1)}, u32[]{:S(2)}, u32[]{:S(2)}) async-start(bf16[64,16,512]{2,1,0:T(8,128)(2,1)} %get-tuple-element.16), calls=%async_computation.3 | async-start | bytes 2097152 | tf_op jit(solution)/shard_map/all_to_all | solution.py:141

commit v2 on v1

--- a/solution.py
+++ b/solution.py
@@ -56,17 +56,31 @@
     t_ref[...] = dot_tn(high, dagg) + dot_tn(low, dagg)
 
 
-def node_kernel(factor, part_ref, w1_ref, cot_ref, high_ref, low_ref, t_ref, grads_ref, dpart_ref):
-    d = w1_ref.shape[0]
+def node_kernel(factor, core_ref, part_ref, w1_ref, cot_ref, high_ref, low_ref, t_ref, keep_ref, send_ref, dpart_ref):
     part = part_ref[...]
     pre = dot(part, w1_ref[...])
     sig = jax.nn.sigmoid(pre)
     act = (pre * sig).astype(BF)
     g = (t_ref[...] * sig * (1.0 + pre * (1.0 - sig))).astype(BF)
+    m = (dot(high_ref[...], act) + dot(low_ref[...], act)).astype(BF)
+    cot = cot_ref[...]
+    zeroth = core_ref[0, 0] == 0
+
+    @pl.when(zeroth)
+    def _():
+        send_ref[...] = (dot_tn(m, cot) * factor).astype(BF)
+        keep_ref[...] = dot_tn(part, g) * factor
+
+    @pl.when(jnp.logical_not(zeroth))
+    def _():
+        send_ref[...] = (dot_tn(part, g) * factor).astype(BF)
+        keep_ref[...] = dot_tn(m, cot) * factor
+
     dpart_ref[...] = dot_nt(g, w1_ref[...]).astype(BF)
-    grads_ref[0:d, :] = (dot_tn(part, g) * factor).astype(BF)
-    m = (dot(high_ref[...], act) + dot(low_ref[...], act)).astype(BF)
-    grads_ref[d : 2 * d, :] = (dot_tn(m, cot_ref[...]) * factor).astype(BF)
+
+
+def add_kernel(keep_ref, got_ref, out_ref):
+    out_ref[...] = (keep_ref[...] + got_ref[...].astype(F32)).astype(BF)
 
 
 def sum_kernel(pieces_ref, dpart_ref, both_ref):
@@ -91,6 +105,13 @@
     out_ref[...] = dot(places, back_ref[...]).astype(BF)
 
 
+def final_kernel(core_ref, mine_ref, other_ref, first_ref, second_ref):
+    zeroth = core_ref[0, 0] == 0
+    mine, other = mine_ref[...].astype(F32), other_ref[...].astype(F32)
+    first_ref[...] = jnp.where(zeroth, mine, other)
+    second_ref[...] = jnp.where(zeroth, other, mine)
+
+
 def call(kernel, out_shape, flops, nbytes, *args, smem=0):
     specs = [pl.BlockSpec(memory_space=pltpu.SMEM)] * smem
     specs += [pl.BlockSpec(memory_space=pltpu.VMEM)] * (len(args) - smem)
@@ -106,15 +127,18 @@
 def shards(grid, cotangent, send_order, tile_nodes, tile_edges, tile_count, w_first, w_second):
     rows, cot, order = grid[0, 0], cotangent[0, 0], send_order[0]
     nodes, edges = tile_nodes[0, 0], tile_edges[0, 0]
-    z = lax.axis_size("grp")
-    rep = lax.axis_size("rep")
+    z = lax.axis_size("z")
+    plane = lax.axis_size("y") * lax.axis_size("x")
+    rep = plane * lax.axis_size("c")
+    core = lax.axis_index("c").reshape(1, 1)
+    swap = [(0, 1), (1, 0)]
     n, d = rows.shape
     most, tile = nodes.shape
     factor = float(z * rep * most * tile) ** -0.5
     sd = jax.ShapeDtypeStruct
 
     outgoing = call(send_kernel, sd((n, d), BF), 2 * n * n * d, 4 * n * d, order, rows)
-    incoming = lax.all_to_all(outgoing.reshape(z, n // z, d), "grp", 0, 0, tiled=True)
+    incoming = lax.all_to_all(outgoing.reshape(z, n // z, d), "z", 0, 0, tiled=True)
     part = incoming.reshape(n, d)
 
     high, low, t = call(
@@ -122,37 +146,49 @@
         (sd((n, n), BF), sd((n, n), BF), sd((n, d), F32)),
         10**9, 6 * 10**6, tile_count, nodes, edges, cot, w_second, smem=1,
     )
-    grads, dpart = call(
+    keep, send, dpart = call(
         lambda *refs: node_kernel(factor, *refs),
-        (sd((2 * d, d), BF), sd((n, d), BF)),
-        5 * 10**8, 3 * 10**6, part, w_first, cot, high, low, t,
+        (sd((d, d), F32), sd((d, d), BF), sd((n, d), BF)),
+        5 * 10**8, 3 * 10**6, core, part, w_first, cot, high, low, t, smem=1,
     )
+    got = lax.ppermute(send, "c", swap)
+    grad = call(add_kernel, sd((d, d), BF), 10**6, 2 * 10**6, keep, got)
 
-    share = 2 * d // rep
-    pieces = lax.all_to_all(grads.reshape(rep, share, d), "rep", 0, 0, tiled=True)
+    share = d // plane
+    pieces = lax.all_to_all(grad.reshape(plane, share, d), ("y", "x"), 0, 0, tiled=True)
     both = call(
         sum_kernel, sd((z, n // z + share, d), BF), 10**6, 2 * 10**6,
         pieces, dpart.reshape(z, n // z, d),
     )
-    both = lax.all_to_all(both, "grp", 0, 0, tiled=True)
+    both = lax.all_to_all(both, "z", 0, 0, tiled=True)
     back, whole = call(
-        spread_kernel, (sd((z, n // z, d), BF), sd((rep, share, d), BF)), 10**6, 2 * 10**6, both
+        spread_kernel, (sd((z, n // z, d), BF), sd((plane, share, d), BF)), 10**6, 2 * 10**6, both
     )
-    whole = lax.all_to_all(whole, "rep", 0, 0, tiled=True).reshape(2 * d, d)
-    grad_rows = call(place_kernel, sd((n, d), BF), 2 * n * n * d, 4 * n * d, order, back.reshape(n, d))
-    return (grad_rows[None, None], whole[:d].astype(F32), whole[d:].astype(F32))
+    mine = lax.all_to_all(whole, ("y", "x"), 0, 0, tiled=True).reshape(d, d)
+    grad_rows = call(
+        place_kernel, sd((n, d), BF), 2 * n * n * d, 4 * n * d, order, back.reshape(n, d)
+    )
+    other = lax.ppermute(mine, "c", swap)
+    first, second = call(
+        final_kernel, (sd((d, d), F32), sd((d, d), F32)), 10**6, 3 * 10**6,
+        core, mine, other, smem=1,
+    )
+    return (grad_rows[None, None], first, second)
 
 
 def solution(mesh):
+    z, rep = mesh.shape["grp"], mesh.shape["rep"]
+    mesh = Mesh(mesh.devices.reshape(z, rep // 8, 4, 2), ("z", "y", "x", "c"))
+    group = ("y", "x", "c")
     in_specs = (
-        P("rep", "grp", None, None),
-        P("rep", "grp", None, None),
-        P("rep", "grp", None),
-        P("rep", "grp", None, None),
-        P("rep", "grp", None, None, None),
-        P("rep", "grp"),
+        P(group, "z", None, None),
+        P(group, "z", None, None),
+        P(group, "z", None),
+        P(group, "z", None, None),
+        P(group, "z", None, None, None),
+        P(group, "z"),
         P(),
         P(),
     )
-    out_specs = (P("rep", "grp", None, None), P(), P())
+    out_specs = (P(group, "z", None, None), P(), P())
     return jax.shard_map(shards, mesh=mesh, in_specs=in_specs, out_specs=out_specs, check_vma=False)

time: 133 us -> 116 us (0.87)
  waiting for transfers between devices: 34.1 us -> 9.78 us
  blocking collectives: 60.3 us -> 66.7 us
  other arithmetic: 1.68 us -> 0 us
  starting transfers between devices: 25.1 us -> 26.6 us
    all_to_all x2 -> x1, waiting for transfers between devices: 34.1 us -> 7.62 us  [shards(): lax.all_to_all(outgoing.reshape(z, n // z, d), 'z', 0, 0, tiled=True)]
    ppermute x0 -> x2, starting transfers between devices: none -> 10.9 us  [the longest x1 6.38 us: shards(): other = lax.ppermute(mine, 'c', swap)]
    all_to_all x2 -> x1, starting transfers between devices: 25.1 us -> 15.7 us  [shards(): lax.all_to_all(outgoing.reshape(z, n // z, d), 'z', 0, 0, tiled=True)]
    all_to_all x2 -> x3, blocking collectives: 60.3 us -> 66.7 us  [the longest x1 26.1 us: shards(): lax.all_to_all(grad.reshape(plane, share, d), ('y', 'x'), 0, 0, tiled=True)]
    ppermute x0 -> x2, waiting for transfers between devices: none -> 2.15 us  [the longest x1 1.51 us: shards(): got = lax.ppermute(send, 'c', swap)]
    convert_element_type x1 -> x0, other arithmetic: 1.68 us -> none  [shards(): return (grad_rows[None, None], whole[:d].astype(F32), whole[d:].astype(F32))]
    pallas_call x6 -> x8, Pallas kernels: 6.09 us -> 6.88 us  [call(): pl.pallas_call(kernel, out_shape=out_shape, in_specs=specs, compiler_para...]
  transfers between devices with their start and end apart: 2 -> 3, of which waited for: 2 -> 3; matrix products, arithmetic and copies ran while one was open for 0% -> 0% of each run, Pallas kernels for 2% -> 2%
where the time goes in v2:
time: 116 us; the launch traced here: 115 us
  blocking collectives  66.7 us (58%)
  starting transfers between devices  26.6 us (23%)
  waiting for transfers between devices  9.78 us (8%)
  Pallas kernels  6.88 us (6%)
  local copies, waits for them, and re-layouts  3.61 us (3%)
  between operations  1.38 us (1%)
    all_to_all x1, blocking collectives, shards(): lax.all_to_all(grad.reshape(plane, share, d), ('y', 'x'), 0, 0, tiled=True)  26.1 us
    all_to_all x1, blocking collectives, shards(): mine = lax.all_to_all(whole, ('y', 'x'), 0, 0, tiled=True).reshape(d, d)  22.2 us
    all_to_all x1, blocking collectives, shards(): both = lax.all_to_all(both, 'z', 0, 0, tiled=True)  18.4 us
    all_to_all x1, starting transfers between devices, shards(): lax.all_to_all(outgoing.reshape(z, n // z, d), 'z', 0, 0, tiled=True)  15.7 us
    all_to_all x1, waiting for transfers between devices, shards(): lax.all_to_all(outgoing.reshape(z, n // z, d), 'z', 0, 0, tiled=True)  7.62 us
    pallas_call x8, Pallas kernels, call(): pl.pallas_call(kernel, out_shape=out_shape, in_specs=specs, compiler_para...  6.88 us
    ppermute x1, starting transfers between devices, shards(): other = lax.ppermute(mine, 'c', swap)  6.38 us
    ppermute x1, starting transfers between devices, shards(): got = lax.ppermute(send, 'c', swap)  4.55 us
  transfers between devices with their start and end apart: 3, of which 3 were waited for; matrix products, arithmetic and copies ran while one was open for 0% of the time, Pallas kernels for 2%

profile of v2, /device:TPU:1, one launch (start us, length us, event | category | flops | bytes accessed | tf_op | source)
XLA Modules:
  0.0 115.0 jit_solution(12307060751296440906)
XLA Ops:
  0.6 0.0 copy-start.1
  0.6 0.7 copy-done.1
  1.3 0.0 copy-start
  1.3 0.9 copy-done
  2.2 0.0 copy-start.2
  2.2 0.9 shard_map.103
  3.2 15.7 %all-to-all-start = ((bf16[12,16,512]{2,1,0:T(8,128)(2,1)}), bf16[12,16,512]{2,1,0:T(8,128)(2,1)S(1)}, u32[]{:S(2)}, u32[]{:S(2)}) async-start(bf16[12,16,512]{2,1,0:T(8,128)(2,1)} %bitcast.3), calls=%async_computation | async-start | bytes 393216 | tf_op jit(solution)/shard_map/all_to_all | solution.py:141
  18.9 0.0 copy-start.7
  19.5 0.0 copy-done.2
  19.5 0.0 copy-done.7
  19.6 0.0 copy-start.3
  19.6 1.0 copy-done.3
  20.6 0.0 copy-start.5
  20.6 0.9 copy-done.5
  21.5 0.0 copy-start.4
  21.5 0.0 copy-start.6
  21.5 1.9 %shard_map.104 = (bf16[192,192]{1,0:T(8,128)(2,1)S(1)}, bf16[192,192]{1,0:T(8,128)(2,1)S(1)}, f32[192,512]{1,0:T(8,128)S(1)}) custom-call(s32[1,1]{1,0:T(1,128)S(6)} %copy.11.count_ref, s32[24,64]{1,0:T(8,128)S(1)} %bitcast.25, s32[24,64,64]{2,1,0:T(8,128)S(1)} %bitcast.22, bf16[192,512]{1,0:T(8,128)(2,1)S(1)} %bitcast.23, bf16[512,512]{1,0:T(8,128)(2,1)S(1)} %copy-done.3), custom_call_target="tpu_custom_call" | custom-call | flops 1000000000 | bytes 6000000 | tf_op jit(solution)/shard_map/pallas_call | solution.py:118
  23.5 7.6 %all-to-all-done = bf16[12,16,512]{2,1,0:T(8,128)(2,1)S(1)} async-done(((bf16[12,16,512]{2,1,0:T(8,128)(2,1)}), bf16[12,16,512]{2,1,0:T(8,128)(2,1)S(1)}, u32[]{:S(2)}, u32[]{:S(2)}) %all-to-all-start) | async-done | bytes 196640 | tf_op jit(solution)/shard_map/all_to_all | solution.py:141
  31.1 0.0 copy-done.4
  31.1 0.0 copy-done.6
  31.1 1.4 %shard_map.105 = (f32[512,512]{1,0:T(8,128)S(1)}, bf16[512,512]{1,0:T(8,128)(2,1)S(1)}, bf16[192,512]{1,0:T(8,128)(2,1)S(1)}) custom-call(s32[1,1]{1,0:T(1,128)} %bitcast.1.refs_0_.core_ref, bf16[192,512]{1,0:T(8,128)(2,1)S(1)} %bitcast.17, bf16[512,512]{1,0:T(8,128)(2,1)S(1)} %copy-done.4, bf16[192,512]{1,0:T(8,128)(2,1)S(1)} %bitcast.24, ...), custom_call_target="tpu_custom_call" | custom-call | flops 500000000 | bytes 3000000 | tf_op jit(solution)/shard_map/pallas_call | solution.py:118
  32.5 4.5 %collective-permute-start = (bf16[512,512]{1,0:T(8,128)(2,1)S(1)}, bf16[512,512]{1,0:T(8,128)(2,1)S(1)}, u32[]{:S(2)}, u32[]{:S(2)}) collective-permute-start(bf16[512,512]{1,0:T(8,128)(2,1)S(1)} %get-tuple-element.17), channel_id=1, source_target_pairs={{0,1},{1,0},{2,3},{3,2},{4,5},{5,4},{6,7},{7,6},{8,9},{9,8},{10,11... | collective-permute-start | bytes 1572872 | tf_op jit(solution)/shard_map/ppermute | solution.py:154
  37.1 1.5 %collective-permute-done.got_ref = bf16[512,512]{1,0:T(8,128)(2,1)S(1)} collective-permute-done((bf16[512,512]{1,0:T(8,128)(2,1)S(1)}, bf16[512,512]{1,0:T(8,128)(2,1)S(1)}, u32[]{:S(2)}, u32[]{:S(2)}) %collective-permute-start) | collective-permute-done | bytes 524320 | tf_op jit(solution)/shard_map/ppermute | solution.py:154
  38.6 0.1 shard_map.106
  38.7 26.1 %all_to_all.20.pieces_ref = bf16[32,16,512]{2,1,0:T(8,128)(2,1)S(1)} all-to-all(bf16[32,16,512]{2,1,0:T(8,128)(2,1)S(1)} %bitcast.15), channel_id=1, replica_groups=mesh['z'=12,'y'=8,'x'=4,'c'=2] {'y','x'}, dimensions={0} | all-to-all | bytes 1048576 | tf_op jit(solution)/shard_map/all_to_all | solution.py:158
  64.8 0.1 shard_map.107
  64.9 18.4 %all_to_all.21.both_ref = bf16[12,32,512]{2,1,0:T(8,128)(2,1)S(1)} all-to-all(bf16[12,32,512]{2,1,0:T(8,128)(2,1)S(1)} %shard_map.107), channel_id=1, replica_groups=mesh['z'=12,'y'=8,'x'=4,'c'=2] {'z'}, dimensions={0} | all-to-all | bytes 786432 | tf_op jit(solution)/shard_map/all_to_all | solution.py:163
  83.3 0.1 shard_map.108
  83.4 22.2 %all_to_all.22 = bf16[32,16,512]{2,1,0:T(8,128)(2,1)S(1)} all-to-all(bf16[32,16,512]{2,1,0:T(8,128)(2,1)S(1)} %get-tuple-element.20), channel_id=1, replica_groups=mesh['z'=12,'y'=8,'x'=4,'c'=2] {'y','x'}, dimensions={0} | all-to-all | bytes 1048576 | tf_op jit(solution)/shard_map/all_to_all | solution.py:167
  105.6 6.4 %collective-permute-start.1 = (bf16[512,512]{1,0:T(8,128)(2,1)S(1)}, bf16[512,512]{1,0:T(8,128)(2,1)S(1)}, u32[]{:S(2)}, u32[]{:S(2)}) collective-permute-start(bf16[512,512]{1,0:T(8,128)(2,1)S(1)} %bitcast.13), channel_id=1, source_target_pairs={{0,1},{1,0},{2,3},{3,2},{4,5},{5,4},{6,7},{7,6},{8,9},{9,8},{10,11... | collective-permute-start | bytes 1572872 | tf_op jit(solution)/shard_map/ppermute | solution.py:171
  112.0 0.9 shard_map.109
  112.9 0.6 collective-permute-done.1.other_ref
  113.5 1.5 %shard_map.110 = (f32[512,512]{1,0:T(8,128)}, f32[512,512]{1,0:T(8,128)}) custom-call(s32[1,1]{1,0:T(1,128)} %bitcast.1.refs_0_.core_ref, bf16[512,512]{1,0:T(8,128)(2,1)S(1)} %bitcast.14, bf16[512,512]{1,0:T(8,128)(2,1)S(1)} %collective-permute-done.1.other_ref), custom_call_target="tpu_custom_call" | custom-call | flops 1000000 | bytes 3000000 | tf_op jit(solution)/shard_map/pallas_call | solution.py:118
Async XLA Ops:
  0.6 0.7 copy-start.1
  1.3 0.9 copy-start
  2.2 17.3 %copy-start.2 = (s32[1,1,24,64,64]{4,3,2,1,0:T(8,128)S(1)}, s32[1,1,24,64,64]{4,3,2,1,0:T(8,128)}, u32[]{:S(2)}) copy-start(s32[1,1,24,64,64]{4,3,2,1,0:T(8,128)} %param.12) | copy-start | bytes 1179652
  3.2 28.0 %all-to-all-start = ((bf16[12,16,512]{2,1,0:T(8,128)(2,1)}), bf16[12,16,512]{2,1,0:T(8,128)(2,1)S(1)}, u32[]{:S(2)}, u32[]{:S(2)}) async-start(bf16[12,16,512]{2,1,0:T(8,128)(2,1)} %bitcast.3), calls=%async_computation | async-start | bytes 393216 | tf_op jit(solution)/shard_map/all_to_all | solution.py:141
  18.9 0.7 copy-start.7
  19.6 1.0 copy-start.3
  20.6 0.9 copy-start.5
  21.5 9.6 %copy-start.4 = (bf16[512,512]{1,0:T(8,128)(2,1)S(1)}, bf16[512,512]{1,0:T(8,128)(2,1)}, u32[]{:S(2)}) copy-start(bf16[512,512]{1,0:T(8,128)(2,1)} %refs_2_.1) | copy-start | bytes 1572868
  21.5 9.6 %copy-start.6 = (bf16[1,1,192,512]{3,2,1,0:T(8,128)(2,1)S(1)}, bf16[1,1,192,512]{3,2,1,0:T(8,128)(2,1)}, u32[]{:S(2)}) copy-start(bf16[1,1,192,512]{3,2,1,0:T(8,128)(2,1)} %param.9) | copy-start | bytes 589828
  32.5 6.1 %collective-permute-start = (bf16[512,512]{1,0:T(8,128)(2,1)S(1)}, bf16[512,512]{1,0:T(8,128)(2,1)S(1)}, u32[]{:S(2)}, u32[]{:S(2)}) collective-permute-start(bf16[512,512]{1,0:T(8,128)(2,1)S(1)} %get-tuple-element.17), channel_id=1, source_target_pairs={{0,1},{1,0},{2,3},{3,2},{4,5},{5,4},{6,7},{7,6},{8,9},{9,8},{10,11... | collective-permute-start | bytes 1572872 | tf_op jit(solution)/shard_map/ppermute | solution.py:154
  105.6 7.9 %collective-permute-start.1 = (bf16[512,512]{1,0:T(8,128)(2,1)S(1)}, bf16[512,512]{1,0:T(8,128)(2,1)S(1)}, u32[]{:S(2)}, u32[]{:S(2)}) collective-permute-start(bf16[512,512]{1,0:T(8,128)(2,1)S(1)} %bitcast.13), channel_id=1, source_target_pairs={{0,1},{1,0},{2,3},{3,2},{4,5},{5,4},{6,7},{7,6},{8,9},{9,8},{10,11... | collective-permute-start | bytes 1572872 | tf_op jit(solution)/shard_map/ppermute | solution.py:171

commit v3 on v2

--- a/solution.py
+++ b/solution.py
@@ -32,9 +32,15 @@
     return high, (a - high.astype(F32)).astype(BF)
 
 
-def send_kernel(order_ref, rows_ref, out_ref):
+def send_kernel(order_hbm, rows_hbm, out_ref, order_ref, rows_ref, sems):
+    order_copy = pltpu.make_async_copy(order_hbm, order_ref, sems.at[0])
+    rows_copy = pltpu.make_async_copy(rows_hbm, rows_ref, sems.at[1])
+    order_copy.start()
+    rows_copy.start()
+    order_copy.wait()
     n = rows_ref.shape[0]
     places = mark(lax.broadcasted_iota(jnp.int32, (n, n), 0) == order_ref[...])
+    rows_copy.wait()
     out_ref[...] = dot_tn(places, rows_ref[...]).astype(BF)
 
 
@@ -80,7 +86,15 @@
 
 
 def add_kernel(keep_ref, got_ref, out_ref):
-    out_ref[...] = (keep_ref[...] + got_ref[...].astype(F32)).astype(BF)
+    nx, ny, share, _ = out_ref.shape
+    for y in range(ny):
+        for x in range(nx):
+            at = pl.ds((y * nx + x) * share, share)
+            out_ref[x, y] = (keep_ref[at, :] + got_ref[at, :].astype(F32)).astype(BF)
+
+
+def sum_x_kernel(pieces_ref, out_ref):
+    out_ref[...] = jnp.sum(pieces_ref[...].astype(F32), axis=0).astype(BF)
 
 
 def sum_kernel(pieces_ref, dpart_ref, both_ref):
@@ -137,7 +151,17 @@
     factor = float(z * rep * most * tile) ** -0.5
     sd = jax.ShapeDtypeStruct
 
-    outgoing = call(send_kernel, sd((n, d), BF), 2 * n * n * d, 4 * n * d, order, rows)
+    outgoing = pl.pallas_call(
+        send_kernel,
+        out_shape=sd((n, d), BF),
+        in_specs=[pl.BlockSpec(memory_space=pl.ANY)] * 2,
+        out_specs=pl.BlockSpec(memory_space=pltpu.VMEM),
+        scratch_shapes=[
+            pltpu.VMEM((1, n), jnp.int32),
+            pltpu.VMEM((n, d), BF),
+            pltpu.SemaphoreType.DMA((2,)),
+        ],
+    )(order, rows)
     incoming = lax.all_to_all(outgoing.reshape(z, n // z, d), "z", 0, 0, tiled=True)
     part = incoming.reshape(n, d)
 
@@ -152,10 +176,14 @@
         5 * 10**8, 3 * 10**6, core, part, w_first, cot, high, low, t, smem=1,
     )
     got = lax.ppermute(send, "c", swap)
-    grad = call(add_kernel, sd((d, d), BF), 10**6, 2 * 10**6, keep, got)
-
+    nx = lax.axis_size("x")
     share = d // plane
-    pieces = lax.all_to_all(grad.reshape(plane, share, d), ("y", "x"), 0, 0, tiled=True)
+    grad = call(
+        add_kernel, sd((nx, plane // nx, share, d), BF), 10**6, 2 * 10**6, keep, got
+    )
+    grad = lax.all_to_all(grad.reshape(nx, d // nx, d), "x", 0, 0, tiled=True)
+    grad = call(sum_x_kernel, sd((d // nx, d), BF), 10**6, 10**6, grad)
+    pieces = lax.all_to_all(grad.reshape(plane // nx, share, d), "y", 0, 0, tiled=True)
     both = call(
         sum_kernel, sd((z, n // z + share, d), BF), 10**6, 2 * 10**6,
         pieces, dpart.reshape(z, n // z, d),

time: 116 us -> 113 us (0.974)
  blocking collectives: 66.7 us -> 61.2 us
  starting transfers between devices: 26.6 us -> 28.5 us
    all_to_all x1, blocking collectives: 22.2 us -> 15.9 us  [shards(): mine = lax.all_to_all(whole, ('y', 'x'), 0, 0, tiled=True).reshape(d, d)]
    pallas_call x0 -> x1, Pallas kernels: none -> 1.94 us  [shards(): pl.pallas_call(send_kernel, out_shape=sd((n, d), BF), in_specs=[pl.BlockS...]
    ppermute x1, starting transfers between devices: 6.38 us -> 8.26 us  [shards(): other = lax.ppermute(mine, 'c', swap)]
    all_to_all x1 -> x2, blocking collectives: 26.1 us -> 27.1 us  [the longest x1 14.6 us: shards(): lax.all_to_all(grad.reshape(plane // nx, share, d), 'y', 0, 0, tiled=True)]
    unnamed x16 -> x14, local copies, waits for them, and re-layouts: 3.61 us -> 2.69 us
  transfers between devices with their start and end apart: 3 -> 3, of which waited for: 3 -> 2; matrix products, arithmetic and copies ran while one was open for 0% -> 0% of each run, Pallas kernels for 2% -> 3%
where the time goes in v3:
time: 113 us; the launch traced here: 111 us
  blocking collectives  61.2 us (54%)
  starting transfers between devices  28.5 us (25%)
  waiting for transfers between devices  9.14 us (8%)
  Pallas kernels  7.89 us (7%)
  local copies, waits for them, and re-layouts  2.69 us (2%)
  between operations  1.39 us (1%)
    all_to_all x1, blocking collectives, shards(): both = lax.all_to_all(both, 'z', 0, 0, tiled=True)  18.2 us
    all_to_all x1, blocking collectives, shards(): mine = lax.all_to_all(whole, ('y', 'x'), 0, 0, tiled=True).reshape(d, d)  15.9 us
    all_to_all x1, starting transfers between devices, shards(): lax.all_to_all(outgoing.reshape(z, n // z, d), 'z', 0, 0, tiled=True)  15.7 us
    all_to_all x1, blocking collectives, shards(): lax.all_to_all(grad.reshape(plane // nx, share, d), 'y', 0, 0, tiled=True)  14.6 us
    all_to_all x1, blocking collectives, shards(): grad = lax.all_to_all(grad.reshape(nx, d // nx, d), 'x', 0, 0, tiled=True)  12.4 us
    ppermute x1, starting transfers between devices, shards(): other = lax.ppermute(mine, 'c', swap)  8.26 us
    all_to_all x1, waiting for transfers between devices, shards(): lax.all_to_all(outgoing.reshape(z, n // z, d), 'z', 0, 0, tiled=True)  7.63 us
    pallas_call x8, Pallas kernels, call(): pl.pallas_call(kernel, out_shape=out_shape, in_specs=specs, compiler_para...  5.95 us
  transfers between devices with their start and end apart: 3, of which 2 were waited for; matrix products, arithmetic and copies ran while one was open for 0% of the time, Pallas kernels for 3%

profile of v3, /device:TPU:1, one launch (start us, length us, event | category | flops | bytes accessed | tf_op | source)
XLA Modules:
  0.0 110.9 jit_solution(12490449862273956539)
XLA Ops:
  0.6 0.0 copy-start.1
  0.6 1.9 %shard_map.103 = bf16[192,512]{1,0:T(8,128)(2,1)} custom-call(s32[1,192]{1,0:T(1,128)} %bitcast.21, bf16[192,512]{1,0:T(8,128)(2,1)} %bitcast.28), custom_call_target="tpu_custom_call" | custom-call | tf_op jit(solution)/shard_map/pallas_call | solution.py:154
  2.6 15.7 %all-to-all-start = ((bf16[12,16,512]{2,1,0:T(8,128)(2,1)}), bf16[12,16,512]{2,1,0:T(8,128)(2,1)S(1)}, u32[]{:S(2)}, u32[]{:S(2)}) async-start(bf16[12,16,512]{2,1,0:T(8,128)(2,1)} %bitcast.27), calls=%async_computation | async-start | bytes 393216 | tf_op jit(solution)/shard_map/all_to_all | solution.py:165
  18.3 0.0 copy-start.6
  19.0 0.0 copy-done.1
  19.0 0.0 copy-done.6
  19.0 0.0 copy-start.2
  19.0 1.0 copy-done.2
  20.1 0.0 copy-start.4
  20.1 0.9 copy-done.4
  21.0 0.0 copy-start.3
  21.0 0.0 copy-start.5
  21.0 1.9 %shard_map.104 = (bf16[192,192]{1,0:T(8,128)(2,1)S(1)}, bf16[192,192]{1,0:T(8,128)(2,1)S(1)}, f32[192,512]{1,0:T(8,128)S(1)}) custom-call(s32[1,1]{1,0:T(1,128)S(6)} %copy.11.count_ref, s32[24,64]{1,0:T(8,128)S(1)} %bitcast.26, s32[24,64,64]{2,1,0:T(8,128)S(1)} %bitcast.23, bf16[192,512]{1,0:T(8,128)(2,1)S(1)} %bitcast.24, bf16[512,512]{1,0:T(8,128)(2,1)S(1)} %copy-done.2), custom_call_target="tpu_custom_call" | custom-call | flops 1000000000 | bytes 6000000 | tf_op jit(solution)/shard_map/pallas_call | solution.py:132
  22.9 7.6 %all-to-all-done = bf16[12,16,512]{2,1,0:T(8,128)(2,1)S(1)} async-done(((bf16[12,16,512]{2,1,0:T(8,128)(2,1)}), bf16[12,16,512]{2,1,0:T(8,128)(2,1)S(1)}, u32[]{:S(2)}, u32[]{:S(2)}) %all-to-all-start) | async-done | bytes 196640 | tf_op jit(solution)/shard_map/all_to_all | solution.py:165
  30.6 0.0 copy-done.3
  30.6 0.0 copy-done.5
  30.6 1.4 %shard_map.105 = (f32[512,512]{1,0:T(8,128)S(1)}, bf16[512,512]{1,0:T(8,128)(2,1)S(1)}, bf16[192,512]{1,0:T(8,128)(2,1)S(1)}) custom-call(s32[1,1]{1,0:T(1,128)} %bitcast.1.refs_0_.core_ref, bf16[192,512]{1,0:T(8,128)(2,1)S(1)} %bitcast.18, bf16[512,512]{1,0:T(8,128)(2,1)S(1)} %copy-done.3, bf16[192,512]{1,0:T(8,128)(2,1)S(1)} %bitcast.25, ...), custom_call_target="tpu_custom_call" | custom-call | flops 500000000 | bytes 3000000 | tf_op jit(solution)/shard_map/pallas_call | solution.py:132
  32.0 4.6 %collective-permute-start = (bf16[512,512]{1,0:T(8,128)(2,1)S(1)}, bf16[512,512]{1,0:T(8,128)(2,1)S(1)}, u32[]{:S(2)}, u32[]{:S(2)}) collective-permute-start(bf16[512,512]{1,0:T(8,128)(2,1)S(1)} %get-tuple-element.17), channel_id=1, source_target_pairs={{0,1},{1,0},{2,3},{3,2},{4,5},{5,4},{6,7},{7,6},{8,9},{9,8},{10,11... | collective-permute-start | bytes 1572872 | tf_op jit(solution)/shard_map/ppermute | solution.py:178
  36.5 1.5 %collective-permute-done.got_ref = bf16[512,512]{1,0:T(8,128)(2,1)S(1)} collective-permute-done((bf16[512,512]{1,0:T(8,128)(2,1)S(1)}, bf16[512,512]{1,0:T(8,128)(2,1)S(1)}, u32[]{:S(2)}, u32[]{:S(2)}) %collective-permute-start) | collective-permute-done | bytes 524320 | tf_op jit(solution)/shard_map/ppermute | solution.py:178
  38.0 0.1 shard_map.106
  38.1 12.4 %all_to_all.25.pieces_ref = bf16[4,128,512]{2,1,0:T(8,128)(2,1)S(1)} all-to-all(bf16[4,128,512]{2,1,0:T(8,128)(2,1)S(1)} %bitcast.16), channel_id=1, replica_groups=mesh['z'=12,'y'=8,'x'=4,'c'=2] {'x'}, dimensions={0} | all-to-all | bytes 1048576 | tf_op jit(solution)/shard_map/all_to_all | solution.py:184
  50.6 0.1 shard_map.107
  50.6 14.6 %all_to_all.26.pieces_ref = bf16[8,16,512]{2,1,0:T(8,128)(2,1)S(1)} all-to-all(bf16[8,16,512]{2,1,0:T(8,128)(2,1)S(1)} %bitcast.17), channel_id=1, replica_groups=mesh['z'=12,'y'=8,'x'=4,'c'=2] {'y'}, dimensions={0} | all-to-all | bytes 262144 | tf_op jit(solution)/shard_map/all_to_all | solution.py:186
  65.3 18.2 %all_to_all.27.both_ref = bf16[12,32,512]{2,1,0:T(8,128)(2,1)S(1)} all-to-all(bf16[12,32,512]{2,1,0:T(8,128)(2,1)S(1)} %shard_map.108), channel_id=1, replica_groups=mesh['z'=12,'y'=8,'x'=4,'c'=2] {'z'}, dimensions={0} | all-to-all | bytes 786432 | tf_op jit(solution)/shard_map/all_to_all | solution.py:191
  83.5 0.1 shard_map.109
  83.6 15.9 %all_to_all.28 = bf16[32,16,512]{2,1,0:T(8,128)(2,1)S(1)} all-to-all(bf16[32,16,512]{2,1,0:T(8,128)(2,1)S(1)} %get-tuple-element.20), channel_id=1, replica_groups=mesh['z'=12,'y'=8,'x'=4,'c'=2] {'y','x'}, dimensions={0} | all-to-all | bytes 1048576 | tf_op jit(solution)/shard_map/all_to_all | solution.py:195
  99.6 8.3 %collective-permute-start.1 = (bf16[512,512]{1,0:T(8,128)(2,1)S(1)}, bf16[512,512]{1,0:T(8,128)(2,1)S(1)}, u32[]{:S(2)}, u32[]{:S(2)}) collective-permute-start(bf16[512,512]{1,0:T(8,128)(2,1)S(1)} %bitcast.14), channel_id=1, source_target_pairs={{0,1},{1,0},{2,3},{3,2},{4,5},{5,4},{6,7},{7,6},{8,9},{9,8},{10,11... | collective-permute-start | bytes 1572872 | tf_op jit(solution)/shard_map/ppermute | solution.py:199
  107.8 0.0 copy-start
  107.8 0.7 copy-done
  108.5 0.9 shard_map.110
  109.4 0.0 collective-permute-done.1.other_ref
  109.4 1.5 %shard_map.111 = (f32[512,512]{1,0:T(8,128)}, f32[512,512]{1,0:T(8,128)}) custom-call(s32[1,1]{1,0:T(1,128)} %bitcast.1.refs_0_.core_ref, bf16[512,512]{1,0:T(8,128)(2,1)S(1)} %bitcast.15, bf16[512,512]{1,0:T(8,128)(2,1)S(1)} %collective-permute-done.1.other_ref), custom_call_target="tpu_custom_call" | custom-call | flops 1000000 | bytes 3000000 | tf_op jit(solution)/shard_map/pallas_call | solution.py:132
  (1 shorter events, 0.0 us)
Async XLA Ops:
  0.6 18.4 %copy-start.1 = (s32[1,1,24,64,64]{4,3,2,1,0:T(8,128)S(1)}, s32[1,1,24,64,64]{4,3,2,1,0:T(8,128)}, u32[]{:S(2)}) copy-start(s32[1,1,24,64,64]{4,3,2,1,0:T(8,128)} %param.12) | copy-start | bytes 1179652
  2.6 28.0 %all-to-all-start = ((bf16[12,16,512]{2,1,0:T(8,128)(2,1)}), bf16[12,16,512]{2,1,0:T(8,128)(2,1)S(1)}, u32[]{:S(2)}, u32[]{:S(2)}) async-start(bf16[12,16,512]{2,1,0:T(8,128)(2,1)} %bitcast.27), calls=%async_computation | async-start | bytes 393216 | tf_op jit(solution)/shard_map/all_to_all | solution.py:165
  18.3 0.7 copy-start.6
  19.0 1.0 copy-start.2
  20.1 0.9 copy-start.4
  21.0 9.6 %copy-start.3 = (bf16[512,512]{1,0:T(8,128)(2,1)S(1)}, bf16[512,512]{1,0:T(8,128)(2,1)}, u32[]{:S(2)}) copy-start(bf16[512,512]{1,0:T(8,128)(2,1)} %refs_2_.1) | copy-start | bytes 1572868
  21.0 9.6 %copy-start.5 = (bf16[1,1,192,512]{3,2,1,0:T(8,128)(2,1)S(1)}, bf16[1,1,192,512]{3,2,1,0:T(8,128)(2,1)}, u32[]{:S(2)}) copy-start(bf16[1,1,192,512]{3,2,1,0:T(8,128)(2,1)} %param.9) | copy-start | bytes 589828
  32.0 6.1 %collective-permute-start = (bf16[512,512]{1,0:T(8,128)(2,1)S(1)}, bf16[512,512]{1,0:T(8,128)(2,1)S(1)}, u32[]{:S(2)}, u32[]{:S(2)}) collective-permute-start(bf16[512,512]{1,0:T(8,128)(2,1)S(1)} %get-tuple-element.17), channel_id=1, source_target_pairs={{0,1},{1,0},{2,3},{3,2},{4,5},{5,4},{6,7},{7,6},{8,9},{9,8},{10,11... | collective-permute-start | bytes 1572872 | tf_op jit(solution)/shard_map/ppermute | solution.py:178
  99.6 9.8 %collective-permute-start.1 = (bf16[512,512]{1,0:T(8,128)(2,1)S(1)}, bf16[512,512]{1,0:T(8,128)(2,1)S(1)}, u32[]{:S(2)}, u32[]{:S(2)}) collective-permute-start(bf16[512,512]{1,0:T(8,128)(2,1)S(1)} %bitcast.14), channel_id=1, source_target_pairs={{0,1},{1,0},{2,3},{3,2},{4,5},{5,4},{6,7},{7,6},{8,9},{9,8},{10,11... | collective-permute-start | bytes 1572872 | tf_op jit(solution)/shard_map/ppermute | solution.py:199
  107.8 0.7 copy-start

commit v4 on v3

--- a/solution.py
+++ b/solution.py
@@ -7,6 +7,7 @@
 
 BF = jnp.bfloat16
 F32 = jnp.float32
+STRIDE = 7
 NT = (((1,), (1,)), ((), ()))
 TN = (((0,), (0,)), ((), ()))
 
@@ -30,6 +31,22 @@
 def split(a):
     high = a.astype(BF)
     return high, (a - high.astype(F32)).astype(BF)
+
+
+def along_z(z):
+    return [STRIDE * k % z for k in range(z)]
+
+
+def in_order(blocks_ref):
+    z = blocks_ref.shape[0]
+    places = along_z(z)
+    return jnp.concatenate([blocks_ref[places.index(k)] for k in range(z)], axis=0)
+
+
+def exchange_z(blocks):
+    return lax.all_to_all(
+        blocks, "z", 0, 0, tiled=True, axis_index_groups=[along_z(blocks.shape[0])]
+    )
 
 
 def send_kernel(order_hbm, rows_hbm, out_ref, order_ref, rows_ref, sems):
@@ -41,7 +58,10 @@
     n = rows_ref.shape[0]
     places = mark(lax.broadcasted_iota(jnp.int32, (n, n), 0) == order_ref[...])
     rows_copy.wait()
-    out_ref[...] = dot_tn(places, rows_ref[...]).astype(BF)
+    sent = dot_tn(places, rows_ref[...]).astype(BF)
+    z, share, _ = out_ref.shape
+    for k, device in enumerate(along_z(z)):
+        out_ref[k] = sent[device * share : (device + 1) * share]
 
 
 def local_kernel(count_ref, nodes_ref, edges_ref, cot_ref, w2_ref, high_ref, low_ref, t_ref):
@@ -62,25 +82,37 @@
     t_ref[...] = dot_tn(high, dagg) + dot_tn(low, dagg)
 
 
-def node_kernel(factor, core_ref, part_ref, w1_ref, cot_ref, high_ref, low_ref, t_ref, keep_ref, send_ref, dpart_ref):
-    part = part_ref[...]
+def node_kernel(factor, core_ref, part_ref, w1_ref, cot_ref, high_ref, low_ref, t_ref, send_ref, g_ref, m_ref):
+    part = in_order(part_ref)
     pre = dot(part, w1_ref[...])
     sig = jax.nn.sigmoid(pre)
     act = (pre * sig).astype(BF)
     g = (t_ref[...] * sig * (1.0 + pre * (1.0 - sig))).astype(BF)
     m = (dot(high_ref[...], act) + dot(low_ref[...], act)).astype(BF)
-    cot = cot_ref[...]
+    g_ref[...] = g
+    m_ref[...] = m
     zeroth = core_ref[0, 0] == 0
 
     @pl.when(zeroth)
     def _():
-        send_ref[...] = (dot_tn(m, cot) * factor).astype(BF)
-        keep_ref[...] = dot_tn(part, g) * factor
+        send_ref[...] = (dot_tn(m, cot_ref[...]) * factor).astype(BF)
 
     @pl.when(jnp.logical_not(zeroth))
     def _():
         send_ref[...] = (dot_tn(part, g) * factor).astype(BF)
-        keep_ref[...] = dot_tn(m, cot) * factor
+
+
+def keep_kernel(factor, core_ref, part_ref, w1_ref, cot_ref, g_ref, m_ref, keep_ref, dpart_ref):
+    zeroth = core_ref[0, 0] == 0
+    g = g_ref[...]
+
+    @pl.when(zeroth)
+    def _():
+        keep_ref[...] = dot_tn(in_order(part_ref), g) * factor
+
+    @pl.when(jnp.logical_not(zeroth))
+    def _():
+        keep_ref[...] = dot_tn(m_ref[...], cot_ref[...]) * factor
 
     dpart_ref[...] = dot_nt(g, w1_ref[...]).astype(BF)
 
@@ -100,14 +132,15 @@
 def sum_kernel(pieces_ref, dpart_ref, both_ref):
     z, share, _ = dpart_ref.shape
     total = jnp.sum(pieces_ref[...].astype(F32), axis=0).astype(BF)
-    for k in range(z):
-        both_ref[k, 0:share, :] = dpart_ref[k]
+    for k, device in enumerate(along_z(z)):
+        both_ref[k, 0:share, :] = dpart_ref[device]
         both_ref[k, share:, :] = total
 
 
 def spread_kernel(both_ref, back_ref, whole_ref):
     z, share, _ = back_ref.shape
-    back_ref[...] = both_ref[:, 0:share, :]
+    for k, device in enumerate(along_z(z)):
+        back_ref[device] = both_ref[k, 0:share, :]
     total = jnp.sum(both_ref[:, share:, :].astype(F32), axis=0).astype(BF)
     for k in range(whole_ref.shape[0]):
         whole_ref[k] = total
@@ -153,7 +186,7 @@
 
     outgoing = pl.pallas_call(
         send_kernel,
-        out_shape=sd((n, d), BF),
+        out_shape=sd((z, n // z, d), BF),
         in_specs=[pl.BlockSpec(memory_space=pl.ANY)] * 2,
         out_specs=pl.BlockSpec(memory_space=pltpu.VMEM),
         scratch_shapes=[
@@ -162,20 +195,24 @@
             pltpu.SemaphoreType.DMA((2,)),
         ],
     )(order, rows)
-    incoming = lax.all_to_all(outgoing.reshape(z, n // z, d), "z", 0, 0, tiled=True)
-    part = incoming.reshape(n, d)
+    part = exchange_z(outgoing)
 
     high, low, t = call(
         local_kernel,
         (sd((n, n), BF), sd((n, n), BF), sd((n, d), F32)),
         10**9, 6 * 10**6, tile_count, nodes, edges, cot, w_second, smem=1,
     )
-    keep, send, dpart = call(
+    send, g, m = call(
         lambda *refs: node_kernel(factor, *refs),
-        (sd((d, d), F32), sd((d, d), BF), sd((n, d), BF)),
-        5 * 10**8, 3 * 10**6, core, part, w_first, cot, high, low, t, smem=1,
+        (sd((d, d), BF), sd((n, d), BF), sd((n, d), BF)),
+        4 * 10**8, 3 * 10**6, core, part, w_first, cot, high, low, t, smem=1,
     )
     got = lax.ppermute(send, "c", swap)
+    keep, dpart = call(
+        lambda *refs: keep_kernel(factor, *refs),
+        (sd((d, d), F32), sd((n, d), BF)),
+        2 * 10**8, 3 * 10**6, core, part, w_first, cot, g, m, smem=1,
+    )
     nx = lax.axis_size("x")
     share = d // plane
     grad = call(
@@ -188,7 +225,7 @@
         sum_kernel, sd((z, n // z + share, d), BF), 10**6, 2 * 10**6,
         pieces, dpart.reshape(z, n // z, d),
     )
-    both = lax.all_to_all(both, "z", 0, 0, tiled=True)
+    both = exchange_z(both)
     back, whole = call(
         spread_kernel, (sd((z, n // z, d), BF), sd((plane, share, d), BF)), 10**6, 2 * 10**6, both
     )

time: 113 us -> 112 us (level)
    unnamed x14 -> x12, local copies, waits for them, and re-layouts: 2.69 us -> 1.84 us
    pallas_call x8 -> x9, Pallas kernels: 5.95 us -> 6.13 us  [call(): pl.pallas_call(kernel, out_shape=out_shape, in_specs=specs, compiler_para...]
where the time goes in v4:
time: 112 us; the launch traced here: 111 us
  blocking collectives  60.5 us (54%)
  starting transfers between devices  29.6 us (26%)
  waiting for transfers between devices  9.56 us (9%)
  Pallas kernels  8.05 us (7%)
  local copies, waits for them, and re-layouts  1.84 us (2%)
  between operations  1.41 us (1%)
    all_to_all x1, blocking collectives, exchange_z(): lax.all_to_all(blocks, 'z', 0, 0, tiled=True, axis_index_groups=[along_z(...  17.5 us
    all_to_all x1, blocking collectives, shards(): mine = lax.all_to_all(whole, ('y', 'x'), 0, 0, tiled=True).reshape(d, d)  15.9 us
    all_to_all x1, starting transfers between devices, exchange_z(): lax.all_to_all(blocks, 'z', 0, 0, tiled=True, axis_index_groups=[along_z(...  15.9 us
    all_to_all x1, blocking collectives, shards(): lax.all_to_all(grad.reshape(plane // nx, share, d), 'y', 0, 0, tiled=True)  14.6 us
    all_to_all x1, blocking collectives, shards(): grad = lax.all_to_all(grad.reshape(nx, d // nx, d), 'x', 0, 0, tiled=True)  12.4 us
    ppermute x1, starting transfers between devices, shards(): other = lax.ppermute(mine, 'c', swap)  9.2 us
    all_to_all x1, waiting for transfers between devices, exchange_z(): lax.all_to_all(blocks, 'z', 0, 0, tiled=True, axis_index_groups=[along_z(...  8.71 us
    pallas_call x9, Pallas kernels, call(): pl.pallas_call(kernel, out_shape=out_shape, in_specs=specs, compiler_para...  6.13 us
  transfers between devices with their start and end apart: 3, of which 2 were waited for; matrix products, arithmetic and copies ran while one was open for 0% of the time, Pallas kernels for 3%

profile of v4, /device:TPU:1, one launch (start us, length us, event | category | flops | bytes accessed | tf_op | source)
XLA Modules:
  0.0 111.0 jit_solution(1417548668861111077)
XLA Ops:
  0.6 0.0 copy-start.4
  0.6 1.9 %shard_map.103 = bf16[12,16,512]{2,1,0:T(8,128)(2,1)} custom-call(s32[1,192]{1,0:T(1,128)} %bitcast.21, bf16[192,512]{1,0:T(8,128)(2,1)} %bitcast.25), custom_call_target="tpu_custom_call" | custom-call | tf_op jit(solution)/shard_map/pallas_call | solution.py:187
  2.6 0.0 copy-start.1
  2.6 15.9 %all-to-all-start = ((bf16[12,16,512]{2,1,0:T(8,128)(2,1)}), bf16[12,16,512]{2,1,0:T(8,128)(2,1)S(1)}, u32[]{:S(2)}, u32[]{:S(2)}) async-start(bf16[12,16,512]{2,1,0:T(8,128)(2,1)} %shard_map.103), calls=%async_computation | async-start | bytes 393216 | tf_op jit(solution)/shard_map/all_to_all | solution.py:47
  18.4 0.0 copy-start.5
  19.1 0.0 copy-done.4
  19.1 0.0 copy-done.1
  19.1 0.0 copy-done.5
  19.2 0.0 copy-start.3
  19.2 1.1 %copy-done.3 = s32[1,1,24,64,64]{4,3,2,1,0:T(8,128)S(1)} copy-done((s32[1,1,24,64,64]{4,3,2,1,0:T(8,128)S(1)}, s32[1,1,24,64,64]{4,3,2,1,0:T(8,128)}, u32[]{:S(2)}) %copy-start.3) | copy-done | bytes 393240
  20.3 0.0 copy-start
  20.3 1.9 %shard_map.104 = (bf16[192,192]{1,0:T(8,128)(2,1)S(1)}, bf16[192,192]{1,0:T(8,128)(2,1)S(1)}, f32[192,512]{1,0:T(8,128)S(1)}) custom-call(s32[1,1]{1,0:T(1,128)S(6)} %copy.11.count_ref, s32[24,64]{1,0:T(8,128)S(1)} %bitcast.24, s32[24,64,64]{2,1,0:T(8,128)S(1)} %bitcast.23, bf16[192,512]{1,0:T(8,128)(2,1)S(1)} %bitcast.15, bf16[512,512]{1,0:T(8,128)(2,1)S(1)} %copy-done.4), custom_call_target="tpu_custom_call" | custom-call | flops 1000000000 | bytes 6000000 | tf_op jit(solution)/shard_map/pallas_call | solution.py:165
  22.2 8.7 %all-to-all-done.refs_1_ = bf16[12,16,512]{2,1,0:T(8,128)(2,1)S(1)} async-done(((bf16[12,16,512]{2,1,0:T(8,128)(2,1)}), bf16[12,16,512]{2,1,0:T(8,128)(2,1)S(1)}, u32[]{:S(2)}, u32[]{:S(2)}) %all-to-all-start) | async-done | bytes 196640 | tf_op jit(solution)/shard_map/all_to_all | solution.py:47
  30.9 0.0 copy-done
  30.9 0.9 shard_map.105
  31.9 4.6 %collective-permute-start = (bf16[512,512]{1,0:T(8,128)(2,1)S(1)}, bf16[512,512]{1,0:T(8,128)(2,1)S(1)}, u32[]{:S(2)}, u32[]{:S(2)}) collective-permute-start(bf16[512,512]{1,0:T(8,128)(2,1)S(1)} %get-tuple-element.21), channel_id=1, source_target_pairs={{0,1},{1,0},{2,3},{3,2},{4,5},{5,4},{6,7},{7,6},{8,9},{9,8},{10,11... | collective-permute-start | bytes 1572872 | tf_op jit(solution)/shard_map/ppermute | solution.py:210
  36.4 0.7 shard_map.106
  37.1 0.8 collective-permute-done.got_ref
  37.9 0.1 shard_map.107
  38.0 12.4 %all_to_all.25.pieces_ref = bf16[4,128,512]{2,1,0:T(8,128)(2,1)S(1)} all-to-all(bf16[4,128,512]{2,1,0:T(8,128)(2,1)S(1)} %bitcast.14), channel_id=1, replica_groups=mesh['z'=12,'y'=8,'x'=4,'c'=2] {'x'}, dimensions={0} | all-to-all | bytes 1048576 | tf_op jit(solution)/shard_map/all_to_all | solution.py:221
  50.5 0.1 shard_map.108
  50.5 14.6 %all_to_all.26.pieces_ref = bf16[8,16,512]{2,1,0:T(8,128)(2,1)S(1)} all-to-all(bf16[8,16,512]{2,1,0:T(8,128)(2,1)S(1)} %bitcast.18), channel_id=1, replica_groups=mesh['z'=12,'y'=8,'x'=4,'c'=2] {'y'}, dimensions={0} | all-to-all | bytes 262144 | tf_op jit(solution)/shard_map/all_to_all | solution.py:223
  65.2 17.5 %all_to_all.27.both_ref = bf16[12,32,512]{2,1,0:T(8,128)(2,1)S(1)} all-to-all(bf16[12,32,512]{2,1,0:T(8,128)(2,1)S(1)} %shard_map.109), channel_id=1, replica_groups={{0,448,128,576,256,704,384,64,512,192,640,320},{1,449,129,577,257,705,3..., dimensions={0} | all-to-all | bytes 786432 | tf_op jit(solution)/shard_map/all_to_all | solution.py:47
  82.7 0.1 shard_map.110
  82.8 15.9 %all_to_all.28 = bf16[32,16,512]{2,1,0:T(8,128)(2,1)S(1)} all-to-all(bf16[32,16,512]{2,1,0:T(8,128)(2,1)S(1)} %get-tuple-element.24), channel_id=1, replica_groups=mesh['z'=12,'y'=8,'x'=4,'c'=2] {'y','x'}, dimensions={0} | all-to-all | bytes 1048576 | tf_op jit(solution)/shard_map/all_to_all | solution.py:232
  98.7 9.2 %collective-permute-start.1 = (bf16[512,512]{1,0:T(8,128)(2,1)S(1)}, bf16[512,512]{1,0:T(8,128)(2,1)S(1)}, u32[]{:S(2)}, u32[]{:S(2)}) collective-permute-start(bf16[512,512]{1,0:T(8,128)(2,1)S(1)} %bitcast.12), channel_id=1, source_target_pairs={{0,1},{1,0},{2,3},{3,2},{4,5},{5,4},{6,7},{7,6},{8,9},{9,8},{10,11... | collective-permute-start | bytes 1572872 | tf_op jit(solution)/shard_map/ppermute | solution.py:236
  107.9 0.0 copy-start.2
  107.9 0.7 copy-done.2
  108.6 0.9 shard_map.111
  109.5 0.0 collective-permute-done.1.other_ref
  109.5 1.5 %shard_map.112 = (f32[512,512]{1,0:T(8,128)}, f32[512,512]{1,0:T(8,128)}) custom-call(s32[1,1]{1,0:T(1,128)} %bitcast.1.refs_0_.core_ref, bf16[512,512]{1,0:T(8,128)(2,1)S(1)} %bitcast.13, bf16[512,512]{1,0:T(8,128)(2,1)S(1)} %collective-permute-done.1.other_ref), custom_call_target="tpu_custom_call" | custom-call | flops 1000000 | bytes 3000000 | tf_op jit(solution)/shard_map/pallas_call | solution.py:165
  (1 shorter events, 0.0 us)
Async XLA Ops:
  0.6 18.5 %copy-start.4 = (bf16[512,512]{1,0:T(8,128)(2,1)S(1)}, bf16[512,512]{1,0:T(8,128)(2,1)}, u32[]{:S(2)}) copy-start(bf16[512,512]{1,0:T(8,128)(2,1)} %w2_ref.1) | copy-start | bytes 1572868
  2.6 16.6 %copy-start.1 = (bf16[1,1,192,512]{3,2,1,0:T(8,128)(2,1)S(1)}, bf16[1,1,192,512]{3,2,1,0:T(8,128)(2,1)}, u32[]{:S(2)}) copy-start(bf16[1,1,192,512]{3,2,1,0:T(8,128)(2,1)} %param.9) | copy-start | bytes 589828
  2.6 28.4 %all-to-all-start = ((bf16[12,16,512]{2,1,0:T(8,128)(2,1)}), bf16[12,16,512]{2,1,0:T(8,128)(2,1)S(1)}, u32[]{:S(2)}, u32[]{:S(2)}) async-start(bf16[12,16,512]{2,1,0:T(8,128)(2,1)} %shard_map.103), calls=%async_computation | async-start | bytes 393216 | tf_op jit(solution)/shard_map/all_to_all | solution.py:47
  18.4 0.7 copy-start.5
  19.2 1.1 %copy-start.3 = (s32[1,1,24,64,64]{4,3,2,1,0:T(8,128)S(1)}, s32[1,1,24,64,64]{4,3,2,1,0:T(8,128)}, u32[]{:S(2)}) copy-start(s32[1,1,24,64,64]{4,3,2,1,0:T(8,128)} %param.12) | copy-start | bytes 1179652
  20.3 10.7 %copy-start = (bf16[512,512]{1,0:T(8,128)(2,1)S(1)}, bf16[512,512]{1,0:T(8,128)(2,1)}, u32[]{:S(2)}) copy-start(bf16[512,512]{1,0:T(8,128)(2,1)} %refs_2_.3) | copy-start | bytes 1572868
  31.9 6.1 %collective-permute-start = (bf16[512,512]{1,0:T(8,128)(2,1)S(1)}, bf16[512,512]{1,0:T(8,128)(2,1)S(1)}, u32[]{:S(2)}, u32[]{:S(2)}) collective-permute-start(bf16[512,512]{1,0:T(8,128)(2,1)S(1)} %get-tuple-element.21), channel_id=1, source_target_pairs={{0,1},{1,0},{2,3},{3,2},{4,5},{5,4},{6,7},{7,6},{8,9},{9,8},{10,11... | collective-permute-start | bytes 1572872 | tf_op jit(solution)/shard_map/ppermute | solution.py:210
  98.7 10.8 %collective-permute-start.1 = (bf16[512,512]{1,0:T(8,128)(2,1)S(1)}, bf16[512,512]{1,0:T(8,128)(2,1)S(1)}, u32[]{:S(2)}, u32[]{:S(2)}) collective-permute-start(bf16[512,512]{1,0:T(8,128)(2,1)S(1)} %bitcast.12), channel_id=1, source_target_pairs={{0,1},{1,0},{2,3},{3,2},{4,5},{5,4},{6,7},{7,6},{8,9},{9,8},{10,11... | collective-permute-start | bytes 1572872 | tf_op jit(solution)/shard_map/ppermute | solution.py:236
  107.9 0.7 copy-start.2

commit v5 on v4

--- a/solution.py
+++ b/solution.py
@@ -7,7 +7,6 @@
 
 BF = jnp.bfloat16
 F32 = jnp.float32
-STRIDE = 7
 NT = (((1,), (1,)), ((), ()))
 TN = (((0,), (0,)), ((), ()))
 
@@ -34,7 +33,8 @@
 
 
 def along_z(z):
-    return [STRIDE * k % z for k in range(z)]
+    half = (z + 1) // 2
+    return [k % 2 * half + k // 2 for k in range(z)]
 
 
 def in_order(blocks_ref):

time: 112 us -> 109 us (0.973)
  starting transfers between devices: 29.6 us -> 33.2 us
  blocking collectives: 60.5 us -> 57.4 us
  waiting for transfers between devices: 9.56 us -> 6.87 us
    all_to_all x1, blocking collectives: 17.5 us -> 14.4 us  [exchange_z(): lax.all_to_all(blocks, 'z', 0, 0, tiled=True, axis_index_groups=[along_z(...]
    all_to_all x1, waiting for transfers between devices: 8.71 us -> 6.02 us  [exchange_z(): lax.all_to_all(blocks, 'z', 0, 0, tiled=True, axis_index_groups=[along_z(...]
    ppermute x1, starting transfers between devices: 4.56 us -> 6.79 us  [shards(): got = lax.ppermute(send, 'c', swap)]
    ppermute x1, starting transfers between devices: 9.2 us -> 10.6 us  [shards(): other = lax.ppermute(mine, 'c', swap)]
where the time goes in v5:
time: 109 us
  blocking collectives  57.4 us (53%)
  starting transfers between devices  33.2 us (30%)
  Pallas kernels  8.05 us (7%)
  waiting for transfers between devices  6.87 us (6%)
  local copies, waits for them, and re-layouts  1.84 us (2%)
  between operations  1.41 us (1%)
    all_to_all x1, blocking collectives, shards(): mine = lax.all_to_all(whole, ('y', 'x'), 0, 0, tiled=True).reshape(d, d)  15.9 us
    all_to_all x1, starting transfers between devices, exchange_z(): lax.all_to_all(blocks, 'z', 0, 0, tiled=True, axis_index_groups=[along_z(...  15.9 us
    all_to_all x1, blocking collectives, shards(): lax.all_to_all(grad.reshape(plane // nx, share, d), 'y', 0, 0, tiled=True)  14.6 us
    all_to_all x1, blocking collectives, exchange_z(): lax.all_to_all(blocks, 'z', 0, 0, tiled=True, axis_index_groups=[along_z(...  14.4 us
    all_to_all x1, blocking collectives, shards(): grad = lax.all_to_all(grad.reshape(nx, d // nx, d), 'x', 0, 0, tiled=True)  12.4 us
    ppermute x1, starting transfers between devices, shards(): other = lax.ppermute(mine, 'c', swap)  10.6 us
    ppermute x1, starting transfers between devices, shards(): got = lax.ppermute(send, 'c', swap)  6.79 us
    pallas_call x9, Pallas kernels, call(): pl.pallas_call(kernel, out_shape=out_shape, in_specs=specs, compiler_para...  6.13 us
  transfers between devices with their start and end apart: 3, of which 2 were waited for; matrix products, arithmetic and copies ran while one was open for 0% of the time, Pallas kernels for 3%

profile of v5, /device:TPU:1, one launch (start us, length us, event | category | flops | bytes accessed | tf_op | source)
XLA Modules:
  0.0 108.8 jit_solution(1677434992825862057)
XLA Ops:
  0.6 0.0 copy-start.4
  0.6 1.9 %shard_map.103 = bf16[12,16,512]{2,1,0:T(8,128)(2,1)} custom-call(s32[1,192]{1,0:T(1,128)} %bitcast.21, bf16[192,512]{1,0:T(8,128)(2,1)} %bitcast.25), custom_call_target="tpu_custom_call" | custom-call | tf_op jit(solution)/shard_map/pallas_call | solution.py:187
  2.6 0.0 copy-start.1
  2.6 15.9 %all-to-all-start = ((bf16[12,16,512]{2,1,0:T(8,128)(2,1)}), bf16[12,16,512]{2,1,0:T(8,128)(2,1)S(1)}, u32[]{:S(2)}, u32[]{:S(2)}) async-start(bf16[12,16,512]{2,1,0:T(8,128)(2,1)} %shard_map.103), calls=%async_computation | async-start | bytes 393216 | tf_op jit(solution)/shard_map/all_to_all | solution.py:47
  18.4 0.0 copy-start.5
  19.1 0.0 copy-done.4
  19.1 0.0 copy-done.1
  19.1 0.0 copy-done.5
  19.2 0.0 copy-start.3
  19.2 1.1 %copy-done.3 = s32[1,1,24,64,64]{4,3,2,1,0:T(8,128)S(1)} copy-done((s32[1,1,24,64,64]{4,3,2,1,0:T(8,128)S(1)}, s32[1,1,24,64,64]{4,3,2,1,0:T(8,128)}, u32[]{:S(2)}) %copy-start.3) | copy-done | bytes 393240
  20.3 0.0 copy-start
  20.3 1.9 %shard_map.104 = (bf16[192,192]{1,0:T(8,128)(2,1)S(1)}, bf16[192,192]{1,0:T(8,128)(2,1)S(1)}, f32[192,512]{1,0:T(8,128)S(1)}) custom-call(s32[1,1]{1,0:T(1,128)S(6)} %copy.11.count_ref, s32[24,64]{1,0:T(8,128)S(1)} %bitcast.24, s32[24,64,64]{2,1,0:T(8,128)S(1)} %bitcast.23, bf16[192,512]{1,0:T(8,128)(2,1)S(1)} %bitcast.15, bf16[512,512]{1,0:T(8,128)(2,1)S(1)} %copy-done.4), custom_call_target="tpu_custom_call" | custom-call | flops 1000000000 | bytes 6000000 | tf_op jit(solution)/shard_map/pallas_call | solution.py:165
  22.2 6.0 %all-to-all-done.refs_1_ = bf16[12,16,512]{2,1,0:T(8,128)(2,1)S(1)} async-done(((bf16[12,16,512]{2,1,0:T(8,128)(2,1)}), bf16[12,16,512]{2,1,0:T(8,128)(2,1)S(1)}, u32[]{:S(2)}, u32[]{:S(2)}) %all-to-all-start) | async-done | bytes 196640 | tf_op jit(solution)/shard_map/all_to_all | solution.py:47
  28.3 0.0 copy-done
  28.3 0.9 shard_map.105
  29.2 6.8 %collective-permute-start = (bf16[512,512]{1,0:T(8,128)(2,1)S(1)}, bf16[512,512]{1,0:T(8,128)(2,1)S(1)}, u32[]{:S(2)}, u32[]{:S(2)}) collective-permute-start(bf16[512,512]{1,0:T(8,128)(2,1)S(1)} %get-tuple-element.21), channel_id=1, source_target_pairs={{0,1},{1,0},{2,3},{3,2},{4,5},{5,4},{6,7},{7,6},{8,9},{9,8},{10,11... | collective-permute-start | bytes 1572872 | tf_op jit(solution)/shard_map/ppermute | solution.py:210
  36.0 0.7 shard_map.106
  36.6 0.8 collective-permute-done.got_ref
  37.5 0.1 shard_map.107
  37.6 12.4 %all_to_all.25.pieces_ref = bf16[4,128,512]{2,1,0:T(8,128)(2,1)S(1)} all-to-all(bf16[4,128,512]{2,1,0:T(8,128)(2,1)S(1)} %bitcast.14), channel_id=1, replica_groups=mesh['z'=12,'y'=8,'x'=4,'c'=2] {'x'}, dimensions={0} | all-to-all | bytes 1048576 | tf_op jit(solution)/shard_map/all_to_all | solution.py:221
  50.0 0.1 shard_map.108
  50.1 14.6 %all_to_all.26.pieces_ref = bf16[8,16,512]{2,1,0:T(8,128)(2,1)S(1)} all-to-all(bf16[8,16,512]{2,1,0:T(8,128)(2,1)S(1)} %bitcast.18), channel_id=1, replica_groups=mesh['z'=12,'y'=8,'x'=4,'c'=2] {'y'}, dimensions={0} | all-to-all | bytes 262144 | tf_op jit(solution)/shard_map/all_to_all | solution.py:223
  64.8 14.4 %all_to_all.27.both_ref = bf16[12,32,512]{2,1,0:T(8,128)(2,1)S(1)} all-to-all(bf16[12,32,512]{2,1,0:T(8,128)(2,1)S(1)} %shard_map.109), channel_id=1, replica_groups={{0,384,64,448,128,512,192,576,256,640,320,704},{1,385,65,449,129,513,19..., dimensions={0} | all-to-all | bytes 786432 | tf_op jit(solution)/shard_map/all_to_all | solution.py:47
  79.2 0.1 shard_map.110
  79.2 15.9 %all_to_all.28 = bf16[32,16,512]{2,1,0:T(8,128)(2,1)S(1)} all-to-all(bf16[32,16,512]{2,1,0:T(8,128)(2,1)S(1)} %get-tuple-element.24), channel_id=1, replica_groups=mesh['z'=12,'y'=8,'x'=4,'c'=2] {'y','x'}, dimensions={0} | all-to-all | bytes 1048576 | tf_op jit(solution)/shard_map/all_to_all | solution.py:232
  95.2 10.6 %collective-permute-start.1 = (bf16[512,512]{1,0:T(8,128)(2,1)S(1)}, bf16[512,512]{1,0:T(8,128)(2,1)S(1)}, u32[]{:S(2)}, u32[]{:S(2)}) collective-permute-start(bf16[512,512]{1,0:T(8,128)(2,1)S(1)} %bitcast.12), channel_id=1, source_target_pairs={{0,1},{1,0},{2,3},{3,2},{4,5},{5,4},{6,7},{7,6},{8,9},{9,8},{10,11... | collective-permute-start | bytes 1572872 | tf_op jit(solution)/shard_map/ppermute | solution.py:236
  105.7 0.0 copy-start.2
  105.7 0.7 copy-done.2
  106.4 0.9 shard_map.111
  107.3 0.0 collective-permute-done.1.other_ref
  107.3 1.5 %shard_map.112 = (f32[512,512]{1,0:T(8,128)}, f32[512,512]{1,0:T(8,128)}) custom-call(s32[1,1]{1,0:T(1,128)} %bitcast.1.refs_0_.core_ref, bf16[512,512]{1,0:T(8,128)(2,1)S(1)} %bitcast.13, bf16[512,512]{1,0:T(8,128)(2,1)S(1)} %collective-permute-done.1.other_ref), custom_call_target="tpu_custom_call" | custom-call | flops 1000000 | bytes 3000000 | tf_op jit(solution)/shard_map/pallas_call | solution.py:165
  (1 shorter events, 0.0 us)
Async XLA Ops:
  0.6 18.5 %copy-start.4 = (bf16[512,512]{1,0:T(8,128)(2,1)S(1)}, bf16[512,512]{1,0:T(8,128)(2,1)}, u32[]{:S(2)}) copy-start(bf16[512,512]{1,0:T(8,128)(2,1)} %w2_ref.1) | copy-start | bytes 1572868
  2.6 16.6 %copy-start.1 = (bf16[1,1,192,512]{3,2,1,0:T(8,128)(2,1)S(1)}, bf16[1,1,192,512]{3,2,1,0:T(8,128)(2,1)}, u32[]{:S(2)}) copy-start(bf16[1,1,192,512]{3,2,1,0:T(8,128)(2,1)} %param.9) | copy-start | bytes 589828
  2.6 25.7 %all-to-all-start = ((bf16[12,16,512]{2,1,0:T(8,128)(2,1)}), bf16[12,16,512]{2,1,0:T(8,128)(2,1)S(1)}, u32[]{:S(2)}, u32[]{:S(2)}) async-start(bf16[12,16,512]{2,1,0:T(8,128)(2,1)} %shard_map.103), calls=%async_computation | async-start | bytes 393216 | tf_op jit(solution)/shard_map/all_to_all | solution.py:47
  18.4 0.7 copy-start.5
  19.2 1.1 %copy-start.3 = (s32[1,1,24,64,64]{4,3,2,1,0:T(8,128)S(1)}, s32[1,1,24,64,64]{4,3,2,1,0:T(8,128)}, u32[]{:S(2)}) copy-start(s32[1,1,24,64,64]{4,3,2,1,0:T(8,128)} %param.12) | copy-start | bytes 1179652
  20.3 8.0 %copy-start = (bf16[512,512]{1,0:T(8,128)(2,1)S(1)}, bf16[512,512]{1,0:T(8,128)(2,1)}, u32[]{:S(2)}) copy-start(bf16[512,512]{1,0:T(8,128)(2,1)} %refs_2_.3) | copy-start | bytes 1572868
  29.2 8.3 %collective-permute-start = (bf16[512,512]{1,0:T(8,128)(2,1)S(1)}, bf16[512,512]{1,0:T(8,128)(2,1)S(1)}, u32[]{:S(2)}, u32[]{:S(2)}) collective-permute-start(bf16[512,512]{1,0:T(8,128)(2,1)S(1)} %get-tuple-element.21), channel_id=1, source_target_pairs={{0,1},{1,0},{2,3},{3,2},{4,5},{5,4},{6,7},{7,6},{8,9},{9,8},{10,11... | collective-permute-start | bytes 1572872 | tf_op jit(solution)/shard_map/ppermute | solution.py:210
  95.2 12.1 %collective-permute-start.1 = (bf16[512,512]{1,0:T(8,128)(2,1)S(1)}, bf16[512,512]{1,0:T(8,128)(2,1)S(1)}, u32[]{:S(2)}, u32[]{:S(2)}) collective-permute-start(bf16[512,512]{1,0:T(8,128)(2,1)S(1)} %bitcast.12), channel_id=1, source_target_pairs={{0,1},{1,0},{2,3},{3,2},{4,5},{5,4},{6,7},{7,6},{8,9},{9,8},{10,11... | collective-permute-start | bytes 1572872 | tf_op jit(solution)/shard_map/ppermute | solution.py:236
  105.7 0.7 copy-start.2

commit v6 on v5

--- a/solution.py
+++ b/solution.py
@@ -32,20 +32,20 @@
     return high, (a - high.astype(F32)).astype(BF)
 
 
-def along_z(z):
+def along(z):
     half = (z + 1) // 2
     return [k % 2 * half + k // 2 for k in range(z)]
 
 
 def in_order(blocks_ref):
     z = blocks_ref.shape[0]
-    places = along_z(z)
+    places = along(z)
     return jnp.concatenate([blocks_ref[places.index(k)] for k in range(z)], axis=0)
 
 
 def exchange_z(blocks):
     return lax.all_to_all(
-        blocks, "z", 0, 0, tiled=True, axis_index_groups=[along_z(blocks.shape[0])]
+        blocks, "z", 0, 0, tiled=True, axis_index_groups=[along(blocks.shape[0])]
     )
 
 
@@ -60,7 +60,7 @@
     rows_copy.wait()
     sent = dot_tn(places, rows_ref[...]).astype(BF)
     z, share, _ = out_ref.shape
-    for k, device in enumerate(along_z(z)):
+    for k, device in enumerate(along(z)):
         out_ref[k] = sent[device * share : (device + 1) * share]
 
 
@@ -119,10 +119,10 @@
 
 def add_kernel(keep_ref, got_ref, out_ref):
     nx, ny, share, _ = out_ref.shape
-    for y in range(ny):
+    for k, y in enumerate(along(ny)):
         for x in range(nx):
             at = pl.ds((y * nx + x) * share, share)
-            out_ref[x, y] = (keep_ref[at, :] + got_ref[at, :].astype(F32)).astype(BF)
+            out_ref[x, k] = (keep_ref[at, :] + got_ref[at, :].astype(F32)).astype(BF)
 
 
 def sum_x_kernel(pieces_ref, out_ref):
@@ -132,14 +132,14 @@
 def sum_kernel(pieces_ref, dpart_ref, both_ref):
     z, share, _ = dpart_ref.shape
     total = jnp.sum(pieces_ref[...].astype(F32), axis=0).astype(BF)
-    for k, device in enumerate(along_z(z)):
+    for k, device in enumerate(along(z)):
         both_ref[k, 0:share, :] = dpart_ref[device]
         both_ref[k, share:, :] = total
 
 
 def spread_kernel(both_ref, back_ref, whole_ref):
     z, share, _ = back_ref.shape
-    for k, device in enumerate(along_z(z)):
+    for k, device in enumerate(along(z)):
         back_ref[device] = both_ref[k, 0:share, :]
     total = jnp.sum(both_ref[:, share:, :].astype(F32), axis=0).astype(BF)
     for k in range(whole_ref.shape[0]):
@@ -152,11 +152,15 @@
     out_ref[...] = dot(places, back_ref[...]).astype(BF)
 
 
-def final_kernel(core_ref, mine_ref, other_ref, first_ref, second_ref):
+def final_kernel(plane, core_ref, mine_ref, other_ref, first_ref, second_ref):
     zeroth = core_ref[0, 0] == 0
-    mine, other = mine_ref[...].astype(F32), other_ref[...].astype(F32)
-    first_ref[...] = jnp.where(zeroth, mine, other)
-    second_ref[...] = jnp.where(zeroth, other, mine)
+    d = mine_ref.shape[0]
+    share = d // plane
+    for k, device in enumerate(along(plane)):
+        at, to = pl.ds(k * share, share), pl.ds(device * share, share)
+        mine, other = mine_ref[at, :].astype(F32), other_ref[at, :].astype(F32)
+        first_ref[to, :] = jnp.where(zeroth, mine, other)
+        second_ref[to, :] = jnp.where(zeroth, other, mine)
 
 
 def call(kernel, out_shape, flops, nbytes, *args, smem=0):
@@ -220,7 +224,9 @@
     )
     grad = lax.all_to_all(grad.reshape(nx, d // nx, d), "x", 0, 0, tiled=True)
     grad = call(sum_x_kernel, sd((d // nx, d), BF), 10**6, 10**6, grad)
-    pieces = lax.all_to_all(grad.reshape(plane // nx, share, d), "y", 0, 0, tiled=True)
+    pieces = lax.all_to_all(
+        grad.reshape(plane // nx, share, d), "y", 0, 0, tiled=True, axis_index_groups=[along(plane // nx)]
+    )
     both = call(
         sum_kernel, sd((z, n // z + share, d), BF), 10**6, 2 * 10**6,
         pieces, dpart.reshape(z, n // z, d),
@@ -229,13 +235,15 @@
     back, whole = call(
         spread_kernel, (sd((z, n // z, d), BF), sd((plane, share, d), BF)), 10**6, 2 * 10**6, both
     )
-    mine = lax.all_to_all(whole, ("y", "x"), 0, 0, tiled=True).reshape(d, d)
+    mine = lax.all_to_all(
+        whole, ("y", "x"), 0, 0, tiled=True, axis_index_groups=[along(plane)]
+    ).reshape(d, d)
     grad_rows = call(
         place_kernel, sd((n, d), BF), 2 * n * n * d, 4 * n * d, order, back.reshape(n, d)
     )
     other = lax.ppermute(mine, "c", swap)
     first, second = call(
-        final_kernel, (sd((d, d), F32), sd((d, d), F32)), 10**6, 3 * 10**6,
+        lambda *refs: final_kernel(plane, *refs), (sd((d, d), F32), sd((d, d), F32)), 10**6, 3 * 10**6,
         core, mine, other, smem=1,
     )
     return (grad_rows[None, None], first, second)

time: 109 us -> 109 us (level)
  blocking collectives: 57.4 us -> 56.2 us
    all_to_all x3, blocking collectives: 45 us -> 43.7 us  [the longest x1 15.9 us: shards(): lax.all_to_all(whole, ('y', 'x'), 0, 0, tiled=True, axis_index_groups=[al...]
where the time goes in v6:
time: 109 us; the launch traced here: 108 us
  blocking collectives  56.2 us (52%)
  starting transfers between devices  33.5 us (31%)
  Pallas kernels  8.04 us (7%)
  waiting for transfers between devices  6.87 us (6%)
  local copies, waits for them, and re-layouts  1.84 us (2%)
  between operations  1.41 us (1%)
    all_to_all x1, blocking collectives, shards(): lax.all_to_all(whole, ('y', 'x'), 0, 0, tiled=True, axis_index_groups=[al...  15.9 us
    all_to_all x1, starting transfers between devices, exchange_z(): lax.all_to_all(blocks, 'z', 0, 0, tiled=True, axis_index_groups=[along(bl...  15.9 us
    all_to_all x1, blocking collectives, exchange_z(): lax.all_to_all(blocks, 'z', 0, 0, tiled=True, axis_index_groups=[along(bl...  14.4 us
    all_to_all x1, blocking collectives, shards(): lax.all_to_all(grad.reshape(plane // nx, share, d), 'y', 0, 0, tiled=True...  13.4 us
    all_to_all x1, blocking collectives, shards(): grad = lax.all_to_all(grad.reshape(nx, d // nx, d), 'x', 0, 0, tiled=True)  12.4 us
    ppermute x1, starting transfers between devices, shards(): other = lax.ppermute(mine, 'c', swap)  10.9 us
    ppermute x1, starting transfers between devices, shards(): got = lax.ppermute(send, 'c', swap)  6.79 us
    pallas_call x9, Pallas kernels, call(): pl.pallas_call(kernel, out_shape=out_shape, in_specs=specs, compiler_para...  6.11 us
  transfers between devices with their start and end apart: 3, of which 2 were waited for; matrix products, arithmetic and copies ran while one was open for 0% of the time, Pallas kernels for 3%

profile of v6, /device:TPU:1, one launch (start us, length us, event | category | flops | bytes accessed | tf_op | source)
XLA Modules:
  0.0 107.8 jit_solution(7803286098099612775)
XLA Ops:
  0.6 0.0 copy-start.4
  0.6 1.9 %shard_map.103 = bf16[12,16,512]{2,1,0:T(8,128)(2,1)} custom-call(s32[1,192]{1,0:T(1,128)} %bitcast.21, bf16[192,512]{1,0:T(8,128)(2,1)} %bitcast.25), custom_call_target="tpu_custom_call" | custom-call | tf_op jit(solution)/shard_map/pallas_call | solution.py:191
  2.6 0.0 copy-start.1
  2.6 15.9 %all-to-all-start = ((bf16[12,16,512]{2,1,0:T(8,128)(2,1)}), bf16[12,16,512]{2,1,0:T(8,128)(2,1)S(1)}, u32[]{:S(2)}, u32[]{:S(2)}) async-start(bf16[12,16,512]{2,1,0:T(8,128)(2,1)} %shard_map.103), calls=%async_computation | async-start | bytes 393216 | tf_op jit(solution)/shard_map/all_to_all | solution.py:47
  18.4 0.0 copy-start.5
  19.1 0.0 copy-done.4
  19.1 0.0 copy-done.1
  19.1 0.0 copy-done.5
  19.2 0.0 copy-start.3
  19.2 1.1 %copy-done.3 = s32[1,1,24,64,64]{4,3,2,1,0:T(8,128)S(1)} copy-done((s32[1,1,24,64,64]{4,3,2,1,0:T(8,128)S(1)}, s32[1,1,24,64,64]{4,3,2,1,0:T(8,128)}, u32[]{:S(2)}) %copy-start.3) | copy-done | bytes 393240
  20.3 0.0 copy-start
  20.3 1.9 %shard_map.104 = (bf16[192,192]{1,0:T(8,128)(2,1)S(1)}, bf16[192,192]{1,0:T(8,128)(2,1)S(1)}, f32[192,512]{1,0:T(8,128)S(1)}) custom-call(s32[1,1]{1,0:T(1,128)S(6)} %copy.11.count_ref, s32[24,64]{1,0:T(8,128)S(1)} %bitcast.24, s32[24,64,64]{2,1,0:T(8,128)S(1)} %bitcast.23, bf16[192,512]{1,0:T(8,128)(2,1)S(1)} %bitcast.15, bf16[512,512]{1,0:T(8,128)(2,1)S(1)} %copy-done.4), custom_call_target="tpu_custom_call" | custom-call | flops 1000000000 | bytes 6000000 | tf_op jit(solution)/shard_map/pallas_call | solution.py:169
  22.2 6.0 %all-to-all-done.refs_1_ = bf16[12,16,512]{2,1,0:T(8,128)(2,1)S(1)} async-done(((bf16[12,16,512]{2,1,0:T(8,128)(2,1)}), bf16[12,16,512]{2,1,0:T(8,128)(2,1)S(1)}, u32[]{:S(2)}, u32[]{:S(2)}) %all-to-all-start) | async-done | bytes 196640 | tf_op jit(solution)/shard_map/all_to_all | solution.py:47
  28.3 0.0 copy-done
  28.3 0.9 shard_map.105
  29.2 6.8 %collective-permute-start = (bf16[512,512]{1,0:T(8,128)(2,1)S(1)}, bf16[512,512]{1,0:T(8,128)(2,1)S(1)}, u32[]{:S(2)}, u32[]{:S(2)}) collective-permute-start(bf16[512,512]{1,0:T(8,128)(2,1)S(1)} %get-tuple-element.21), channel_id=1, source_target_pairs={{0,1},{1,0},{2,3},{3,2},{4,5},{5,4},{6,7},{7,6},{8,9},{9,8},{10,11... | collective-permute-start | bytes 1572872 | tf_op jit(solution)/shard_map/ppermute | solution.py:214
  36.0 0.7 shard_map.106
  36.6 0.8 collective-permute-done.got_ref
  37.5 0.1 shard_map.107
  37.6 12.4 %all_to_all.25.pieces_ref = bf16[4,128,512]{2,1,0:T(8,128)(2,1)S(1)} all-to-all(bf16[4,128,512]{2,1,0:T(8,128)(2,1)S(1)} %bitcast.14), channel_id=1, replica_groups=mesh['z'=12,'y'=8,'x'=4,'c'=2] {'x'}, dimensions={0} | all-to-all | bytes 1048576 | tf_op jit(solution)/shard_map/all_to_all | solution.py:225
  50.0 0.1 shard_map.108
  50.1 13.4 %all_to_all.26.pieces_ref = bf16[8,16,512]{2,1,0:T(8,128)(2,1)S(1)} all-to-all(bf16[8,16,512]{2,1,0:T(8,128)(2,1)S(1)} %bitcast.18), channel_id=1, replica_groups={{0,32,8,40,16,48,24,56},{1,33,9,41,17,49,25,57},{2,34,10,42,18,50,26,58..., dimensions={0} | all-to-all | bytes 262144 | tf_op jit(solution)/shard_map/all_to_all | solution.py:227
  63.5 14.4 %all_to_all.27.both_ref = bf16[12,32,512]{2,1,0:T(8,128)(2,1)S(1)} all-to-all(bf16[12,32,512]{2,1,0:T(8,128)(2,1)S(1)} %shard_map.109), channel_id=1, replica_groups={{0,384,64,448,128,512,192,576,256,640,320,704},{1,385,65,449,129,513,19..., dimensions={0} | all-to-all | bytes 786432 | tf_op jit(solution)/shard_map/all_to_all | solution.py:47
  77.9 0.1 shard_map.110
  78.0 15.9 %all_to_all.28 = bf16[32,16,512]{2,1,0:T(8,128)(2,1)S(1)} all-to-all(bf16[32,16,512]{2,1,0:T(8,128)(2,1)S(1)} %get-tuple-element.24), channel_id=1, replica_groups={{0,32,2,34,4,36,6,38,8,40,10,42,12,44,14,46,16,48,18,50,20,52,22,54,24,..., dimensions={0} | all-to-all | bytes 1048576 | tf_op jit(solution)/shard_map/all_to_all | solution.py:238
  93.9 10.9 %collective-permute-start.1 = (bf16[512,512]{1,0:T(8,128)(2,1)S(1)}, bf16[512,512]{1,0:T(8,128)(2,1)S(1)}, u32[]{:S(2)}, u32[]{:S(2)}) collective-permute-start(bf16[512,512]{1,0:T(8,128)(2,1)S(1)} %bitcast.12), channel_id=1, source_target_pairs={{0,1},{1,0},{2,3},{3,2},{4,5},{5,4},{6,7},{7,6},{8,9},{9,8},{10,11... | collective-permute-start | bytes 1572872 | tf_op jit(solution)/shard_map/ppermute | solution.py:244
  104.8 0.0 copy-start.2
  104.8 0.7 copy-done.2
  105.5 0.9 shard_map.111
  106.4 0.0 collective-permute-done.1.refs_2_
  106.4 1.5 %shard_map.112 = (f32[512,512]{1,0:T(8,128)}, f32[512,512]{1,0:T(8,128)}) custom-call(s32[1,1]{1,0:T(1,128)} %bitcast.1.refs_0_, bf16[512,512]{1,0:T(8,128)(2,1)S(1)} %bitcast.13, bf16[512,512]{1,0:T(8,128)(2,1)S(1)} %collective-permute-done.1.refs_2_), custom_call_target="tpu_custom_call" | custom-call | flops 1000000 | bytes 3000000 | tf_op jit(solution)/shard_map/pallas_call | solution.py:169
  (1 shorter events, 0.0 us)
Async XLA Ops:
  0.6 18.5 %copy-start.4 = (bf16[512,512]{1,0:T(8,128)(2,1)S(1)}, bf16[512,512]{1,0:T(8,128)(2,1)}, u32[]{:S(2)}) copy-start(bf16[512,512]{1,0:T(8,128)(2,1)} %w2_ref.1) | copy-start | bytes 1572868
  2.6 16.6 %copy-start.1 = (bf16[1,1,192,512]{3,2,1,0:T(8,128)(2,1)S(1)}, bf16[1,1,192,512]{3,2,1,0:T(8,128)(2,1)}, u32[]{:S(2)}) copy-start(bf16[1,1,192,512]{3,2,1,0:T(8,128)(2,1)} %param.9) | copy-start | bytes 589828
  2.6 25.7 %all-to-all-start = ((bf16[12,16,512]{2,1,0:T(8,128)(2,1)}), bf16[12,16,512]{2,1,0:T(8,128)(2,1)S(1)}, u32[]{:S(2)}, u32[]{:S(2)}) async-start(bf16[12,16,512]{2,1,0:T(8,128)(2,1)} %shard_map.103), calls=%async_computation | async-start | bytes 393216 | tf_op jit(solution)/shard_map/all_to_all | solution.py:47
  18.4 0.7 copy-start.5
  19.2 1.1 %copy-start.3 = (s32[1,1,24,64,64]{4,3,2,1,0:T(8,128)S(1)}, s32[1,1,24,64,64]{4,3,2,1,0:T(8,128)}, u32[]{:S(2)}) copy-start(s32[1,1,24,64,64]{4,3,2,1,0:T(8,128)} %param.12) | copy-start | bytes 1179652
  20.3 8.0 %copy-start = (bf16[512,512]{1,0:T(8,128)(2,1)S(1)}, bf16[512,512]{1,0:T(8,128)(2,1)}, u32[]{:S(2)}) copy-start(bf16[512,512]{1,0:T(8,128)(2,1)} %refs_2_.3) | copy-start | bytes 1572868
  29.2 8.3 %collective-permute-start = (bf16[512,512]{1,0:T(8,128)(2,1)S(1)}, bf16[512,512]{1,0:T(8,128)(2,1)S(1)}, u32[]{:S(2)}, u32[]{:S(2)}) collective-permute-start(bf16[512,512]{1,0:T(8,128)(2,1)S(1)} %get-tuple-element.21), channel_id=1, source_target_pairs={{0,1},{1,0},{2,3},{3,2},{4,5},{5,4},{6,7},{7,6},{8,9},{9,8},{10,11... | collective-permute-start | bytes 1572872 | tf_op jit(solution)/shard_map/ppermute | solution.py:214
  93.9 12.5 %collective-permute-start.1 = (bf16[512,512]{1,0:T(8,128)(2,1)S(1)}, bf16[512,512]{1,0:T(8,128)(2,1)S(1)}, u32[]{:S(2)}, u32[]{:S(2)}) collective-permute-start(bf16[512,512]{1,0:T(8,128)(2,1)S(1)} %bitcast.12), channel_id=1, source_target_pairs={{0,1},{1,0},{2,3},{3,2},{4,5},{5,4},{6,7},{7,6},{8,9},{9,8},{10,11... | collective-permute-start | bytes 1572872 | tf_op jit(solution)/shard_map/ppermute | solution.py:244
  104.8 0.7 copy-start.2
